TPU v7x, 32 devices: a whole 2x2x4 slice. The times are simulated.
32 devices in a mesh: img: 16 (over z, x, core), seq: 2 (over y).
Axes of the slice: x: 2, y: 2, z: 4, core: 2. Of those that a mesh axis runs over, the one named last changes fastest.
Arguments:
- patches: bfloat16 [64, 1024, 768], P('img', 'seq'), may hold values from -6 to 6
- lengths: int32 [64], P('img'), may hold values from 192 to 1024, as said below
- pooled_cot: float32 [64, 768], P('img'), may hold values from -6 to 6
- norm1_gain: bfloat16 [768], P(('img', 'seq')), may hold values from 0.5 to 1.5
- norm1_bias: bfloat16 [768], P(('img', 'seq')), may hold values from -1.75 to 1.75
- qkv_weight: bfloat16 [768, 2304], P(('img', 'seq')), may hold values from -0.21875 to 0.21875
- query_bias: bfloat16 [768], P(('img', 'seq')), may hold values from -1.75 to 1.75
- value_bias: bfloat16 [768], P(('img', 'seq')), may hold values from -1.75 to 1.75
- attn_weight: bfloat16 [768, 768], P(('img', 'seq')), may hold values from -1.25 to 1.25
- attn_bias: bfloat16 [768], P(('img', 'seq')), may hold values from -1.75 to 1.75
- norm2_gain: bfloat16 [768], P(('img', 'seq')), may hold values from 0.5 to 1.5
- norm2_bias: bfloat16 [768], P(('img', 'seq')), may hold values from -1.75 to 1.75
- fc1_weight: bfloat16 [768, 3072], P(('img', 'seq')), may hold values from -0.21875 to 0.21875
- fc1_bias: bfloat16 [3072], P(('img', 'seq')), may hold values from -1.75 to 1.75
- fc2_weight: bfloat16 [3072, 768], P(('img', 'seq')), may hold values from -0.109375 to 0.109375
- fc2_bias: bfloat16 [768], P(('img', 'seq')), may hold values from -1.75 to 1.75
- final_gain: bfloat16 [768], P(('img', 'seq')), may hold values from 0.5 to 1.5
- final_bias: bfloat16 [768], P(('img', 'seq')), may hold values from -1.75 to 1.75
- probe_vector: bfloat16 [768], P(('img', 'seq')), may hold values from -6 to 6
- pool_query_weight: bfloat16 [768, 768], P(('img', 'seq')), may hold values from -0.21875 to 0.21875
- pool_query_bias: bfloat16 [768], P(('img', 'seq')), may hold values from -1.75 to 1.75
- pool_kv_weight: bfloat16 [768, 1536], P(('img', 'seq')), may hold values from -0.21875 to 0.21875
- pool_value_bias: bfloat16 [768], P(('img', 'seq')), may hold values from -1.75 to 1.75
- pool_out_weight: bfloat16 [768, 768], P(('img', 'seq')), may hold values from -1.25 to 1.25
- pool_out_bias: bfloat16 [768], P(('img', 'seq')), may hold values from -1.75 to 1.75
- head_gain: bfloat16 [768], P(('img', 'seq')), may hold values from 0.5 to 1.5
- head_bias: bfloat16 [768], P(('img', 'seq')), may hold values from -1.75 to 1.75
- head_fc1_weight: bfloat16 [768, 3072], P(('img', 'seq')), may hold values from -0.21875 to 0.21875
- head_fc1_bias: bfloat16 [3072], P(('img', 'seq')), may hold values from -1.75 to 1.75
- head_fc2_weight: bfloat16 [3072, 768], P(('img', 'seq')), may hold values from -0.109375 to 0.109375
- head_fc2_bias: bfloat16 [768], P(('img', 'seq')), may hold values from -1.75 to 1.75
Outputs:
- pooled: float32 [64, 768], P('img')
- patch_grad: float32 [64, 1024, 768], P('img', 'seq')
- grad_norm1_gain: float32 [768], P(('img', 'seq'))
- grad_norm1_bias: float32 [768], P(('img', 'seq'))
- grad_qkv_weight: float32 [768, 2304], P(('img', 'seq'))
- grad_query_bias: float32 [768], P(('img', 'seq'))
- grad_value_bias: float32 [768], P(('img', 'seq'))
- grad_attn_weight: float32 [768, 768], P(('img', 'seq'))
- grad_attn_bias: float32 [768], P(('img', 'seq'))
- grad_norm2_gain: float32 [768], P(('img', 'seq'))
- grad_norm2_bias: float32 [768], P(('img', 'seq'))
- grad_fc1_weight: float32 [768, 3072], P(('img', 'seq'))
- grad_fc1_bias: float32 [3072], P(('img', 'seq'))
- grad_fc2_weight: float32 [3072, 768], P(('img', 'seq'))
- grad_fc2_bias: float32 [768], P(('img', 'seq'))
- grad_final_gain: float32 [768], P(('img', 'seq'))
- grad_final_bias: float32 [768], P(('img', 'seq'))
- grad_probe_vector: float32 [768], P(('img', 'seq'))
- grad_pool_query_weight: float32 [768, 768], P(('img', 'seq'))
- grad_pool_query_bias: float32 [768], P(('img', 'seq'))
- grad_pool_kv_weight: float32 [768, 1536], P(('img', 'seq'))
- grad_pool_value_bias: float32 [768], P(('img', 'seq'))
- grad_pool_out_weight: float32 [768, 768], P(('img', 'seq'))
- grad_pool_out_bias: float32 [768], P(('img', 'seq'))
- grad_head_gain: float32 [768], P(('img', 'seq'))
- grad_head_bias: float32 [768], P(('img', 'seq'))
- grad_head_fc1_weight: float32 [768, 3072], P(('img', 'seq'))
- grad_head_fc1_bias: float32 [3072], P(('img', 'seq'))
- grad_head_fc2_weight: float32 [3072, 768], P(('img', 'seq'))
- grad_head_fc2_bias: float32 [768], P(('img', 'seq'))
Inputs may be any that keep to these rules, and one draw needn't show every extreme that they name: `lengths`: valid patches of each image; positions from the count on are padding.
All inputs are finite; a program needn't handle non-finite values.
Results may differ from a plain program's by a relative error of at most 0.024.
Values may be sent and summed in bfloat16 or wider, within the bound.
No kernel may reach another device: no remote copies, remote signals or barrier semaphores. Data moves between devices by JAX's collectives and lax.ppermute only.
A program may use at most 320 MiB of HBM per device.

v0:
```python
import jax
import jax.numpy as jnp
from jax import lax
from jax.sharding import PartitionSpec as P

HEADS = 12
LEN = 1024


highest = lax.Precision.HIGHEST
masked_score = -1e30
norm_epsilon = 1e-06
wide_type = jnp.float32
narrow_type = jnp.bfloat16


def combined_all(value, axis, join):
    pieces = jax.tree.map(lambda part: lax.all_gather(part, axis), value)
    head = jax.tree.map(lambda part: part[0], pieces)
    tail = jax.tree.map(lambda part: part[1:], pieces)
    subtotal, _ = lax.scan(lambda subtotal, slab: (join(subtotal, slab), None), head, tail)
    return subtotal


def layer_norm(source, norm_gain, norm_bias):
    centre = jnp.mean(source, axis=-1, keepdims=True)
    centred = source - centre
    spread = jnp.mean(centred * centred, axis=-1, keepdims=True)
    return centred * lax.rsqrt(spread + norm_epsilon) * norm_gain + norm_bias


def gelu_tanh(source):
    return jax.nn.gelu(source, approximate=True)


def dense(left_op, right_op):
    return jnp.dot(left_op, right_op, preferred_element_type=wide_type)


def outer_sum(left_op, right_op):
    return lax.dot_general(
        left_op, right_op, (((0,), (0,)), ((), ())), preferred_element_type=wide_type
    )


def back_dense(left_op, right_op):
    return lax.dot_general(
        left_op, right_op, (((1,), (1,)), ((), ())), preferred_element_type=wide_type
    )


def combine_parts(first, second):
    first_top, first_total, first_sum = first
    second_top, second_total, second_sum = second
    joint_top = jnp.maximum(first_top, second_top)
    first_scale = jnp.exp(first_top - joint_top)
    second_scale = jnp.exp(second_top - joint_top)
    joint_total = first_total * first_scale + second_total * second_scale
    joint_sum = first_sum * first_scale[..., None] + second_sum * second_scale[..., None]
    return (joint_top, joint_total, joint_sum)


def local(
    patches,
    lengths,
    pooled_cot,
    norm1_gain,
    norm1_bias,
    qkv_weight,
    query_bias,
    value_bias,
    attn_weight,
    attn_bias,
    norm2_gain,
    norm2_bias,
    fc1_weight,
    fc1_bias,
    fc2_weight,
    fc2_bias,
    final_gain,
    final_bias,
    probe_vector,
    pool_query_weight,
    pool_query_bias,
    pool_kv_weight,
    pool_value_bias,
    pool_out_weight,
    pool_out_bias,
    head_gain,
    head_bias,
    head_fc1_weight,
    head_fc1_bias,
    head_fc2_weight,
    head_fc2_bias,
):
    (
        norm1_gain,
        norm1_bias,
        qkv_weight,
        query_bias,
        value_bias,
        attn_weight,
        attn_bias,
        norm2_gain,
        norm2_bias,
        fc1_weight,
        fc1_bias,
        fc2_weight,
        fc2_bias,
        final_gain,
        final_bias,
        probe_vector,
        pool_query_weight,
        pool_query_bias,
        pool_kv_weight,
        pool_value_bias,
        pool_out_weight,
        pool_out_bias,
        head_gain,
        head_bias,
        head_fc1_weight,
        head_fc1_bias,
        head_fc2_weight,
        head_fc2_bias,
    ) = (
        lax.all_gather(norm1_gain, ("img", "seq"), axis=0, tiled=True),
        lax.all_gather(norm1_bias, ("img", "seq"), axis=0, tiled=True),
        lax.all_gather(qkv_weight, ("img", "seq"), axis=0, tiled=True),
        lax.all_gather(query_bias, ("img", "seq"), axis=0, tiled=True),
        lax.all_gather(value_bias, ("img", "seq"), axis=0, tiled=True),
        lax.all_gather(attn_weight, ("img", "seq"), axis=0, tiled=True),
        lax.all_gather(attn_bias, ("img", "seq"), axis=0, tiled=True),
        lax.all_gather(norm2_gain, ("img", "seq"), axis=0, tiled=True),
        lax.all_gather(norm2_bias, ("img", "seq"), axis=0, tiled=True),
        lax.all_gather(fc1_weight, ("img", "seq"), axis=0, tiled=True),
        lax.all_gather(fc1_bias, ("img", "seq"), axis=0, tiled=True),
        lax.all_gather(fc2_weight, ("img", "seq"), axis=0, tiled=True),
        lax.all_gather(fc2_bias, ("img", "seq"), axis=0, tiled=True),
        lax.all_gather(final_gain, ("img", "seq"), axis=0, tiled=True),
        lax.all_gather(final_bias, ("img", "seq"), axis=0, tiled=True),
        lax.all_gather(probe_vector, ("img", "seq"), axis=0, tiled=True),
        lax.all_gather(pool_query_weight, ("img", "seq"), axis=0, tiled=True),
        lax.all_gather(pool_query_bias, ("img", "seq"), axis=0, tiled=True),
        lax.all_gather(pool_kv_weight, ("img", "seq"), axis=0, tiled=True),
        lax.all_gather(pool_value_bias, ("img", "seq"), axis=0, tiled=True),
        lax.all_gather(pool_out_weight, ("img", "seq"), axis=0, tiled=True),
        lax.all_gather(pool_out_bias, ("img", "seq"), axis=0, tiled=True),
        lax.all_gather(head_gain, ("img", "seq"), axis=0, tiled=True),
        lax.all_gather(head_bias, ("img", "seq"), axis=0, tiled=True),
        lax.all_gather(head_fc1_weight, ("img", "seq"), axis=0, tiled=True),
        lax.all_gather(head_fc1_bias, ("img", "seq"), axis=0, tiled=True),
        lax.all_gather(head_fc2_weight, ("img", "seq"), axis=0, tiled=True),
        lax.all_gather(head_fc2_bias, ("img", "seq"), axis=0, tiled=True),
    )
    groups, block_rows, model_width = patches.shape
    row_count = groups * block_rows
    head_dim = model_width // HEADS
    seq_index = lax.axis_index("seq")
    leader = (seq_index == 0).astype(wide_type)

    def split_heads(source):
        return source.reshape(source.shape[0], HEADS, head_dim)

    def scores_of(query_rows, key_rows, valid_keys):
        scores = (
            jnp.einsum(
                "qhd,khd->hqk",
                split_heads(query_rows),
                split_heads(key_rows),
                preferred_element_type=wide_type,
            )
            * 0.125
        )
        return jnp.where(valid_keys[None, None, :], scores, masked_score)

    flat_rows = patches.reshape(row_count, model_width).astype(wide_type)
    normed1, norm1_pull = jax.vjp(
        layer_norm, flat_rows, norm1_gain.astype(wide_type), norm1_bias.astype(wide_type)
    )
    normed1_low = normed1.astype(narrow_type)
    qkv_rows = dense(normed1_low, qkv_weight)
    queries = (qkv_rows[:, :model_width] + query_bias.astype(wide_type)).astype(narrow_type)
    key_rows = qkv_rows[:, model_width : 2 * model_width].astype(narrow_type)
    values = (qkv_rows[:, 2 * model_width :] + value_bias.astype(wide_type)).astype(narrow_type)
    query_blocks = queries.reshape(groups, block_rows, model_width)
    key_blocks = key_rows.reshape(groups, block_rows, model_width)
    value_blocks = values.reshape(groups, block_rows, model_width)
    key_whole, value_whole = (
        lax.all_gather(key_blocks, "seq", axis=1, tiled=True),
        lax.all_gather(value_blocks, "seq", axis=1, tiled=True),
    )
    key_valid = jnp.arange(LEN)[None, :] < lengths[:, None]
    own_valid = (seq_index * block_rows + jnp.arange(block_rows))[None, :] < lengths[:, None]

    def attend(inputs):
        query_rows, whole_keys, whole_values, valid_keys = inputs
        scores = scores_of(query_rows, whole_keys, valid_keys)
        top_score = jnp.max(scores, axis=-1, keepdims=True)
        raised = jnp.exp(scores - top_score)
        row_total = jnp.sum(raised, axis=-1, keepdims=True)
        shares = (raised / row_total).astype(narrow_type)
        attended = jnp.einsum(
            "hqk,khd->qhd", shares, split_heads(whole_values), preferred_element_type=wide_type
        )
        return (attended.reshape(-1, model_width), (top_score + jnp.log(row_total))[:, :, 0])

    attended, log_sums = lax.map(attend, (query_blocks, key_whole, value_whole, key_valid))
    attended_low = attended.reshape(row_count, model_width).astype(narrow_type)
    branch = dense(attended_low, attn_weight) + attn_bias.astype(wide_type)
    residual = flat_rows + branch
    normed2, norm2_pull = jax.vjp(
        layer_norm, residual, norm2_gain.astype(wide_type), norm2_bias.astype(wide_type)
    )
    normed2_low = normed2.astype(narrow_type)
    hidden_pre = dense(normed2_low, fc1_weight) + fc1_bias.astype(wide_type)
    hidden_wide, hidden_pull = jax.vjp(gelu_tanh, hidden_pre)
    hidden_act = hidden_wide.astype(narrow_type)
    encoded = residual + dense(hidden_act, fc2_weight) + fc2_bias.astype(wide_type)
    final_norm, final_pull = jax.vjp(
        layer_norm, encoded, final_gain.astype(wide_type), final_bias.astype(wide_type)
    )
    final_low = final_norm.astype(narrow_type)
    pool_query = (
        dense(probe_vector[None, :], pool_query_weight)[0] + pool_query_bias.astype(wide_type)
    ).astype(narrow_type)
    pool_kv = dense(final_low, pool_kv_weight)
    pool_keys = (
        pool_kv[:, :model_width].astype(narrow_type).reshape(groups, block_rows, HEADS, head_dim)
    )
    pool_values = (pool_kv[:, model_width:] + pool_value_bias.astype(wide_type)).astype(narrow_type)
    pool_values = pool_values.reshape(groups, block_rows, HEADS, head_dim)
    pool_scores = (
        jnp.einsum(
            "gbhd,hd->ghb",
            pool_keys,
            pool_query.reshape(HEADS, head_dim),
            preferred_element_type=wide_type,
        )
        * 0.125
    )
    pool_scores = jnp.where(own_valid[:, None, :], pool_scores, masked_score)
    local_top = jnp.max(pool_scores, axis=-1)
    local_raised = jnp.where(
        own_valid[:, None, :], jnp.exp(pool_scores - local_top[..., None]), 0.0
    )
    local_total = jnp.sum(local_raised, axis=-1)
    values_wide = pool_values.astype(wide_type)
    local_sum = jnp.einsum("ghb,gbhd->ghd", local_raised, values_wide, precision=highest)
    pool_top, pool_total, pool_sum = combined_all(
        (local_top, local_total, local_sum), "seq", combine_parts
    )
    pooled_heads = pool_sum / pool_total[..., None]
    pool_log = pool_top + jnp.log(pool_total)
    pooled_low = pooled_heads.reshape(groups, model_width).astype(narrow_type)
    pool_branch = dense(pooled_low, pool_out_weight) + pool_out_bias.astype(wide_type)
    head_normed, head_norm_pull = jax.vjp(
        layer_norm, pool_branch, head_gain.astype(wide_type), head_bias.astype(wide_type)
    )
    head_low = head_normed.astype(narrow_type)
    head_pre = dense(head_low, head_fc1_weight) + head_fc1_bias.astype(wide_type)
    head_wide, head_gelu_pull = jax.vjp(gelu_tanh, head_pre)
    head_act = head_wide.astype(narrow_type)
    pooled = pool_branch + dense(head_act, head_fc2_weight) + head_fc2_bias.astype(wide_type)
    cot_low = pooled_cot.astype(narrow_type)
    grad_head_fc2_weight = outer_sum(head_act, cot_low) * leader
    grad_head_fc2_bias = jnp.sum(cot_low.astype(wide_type), axis=0) * leader
    head_pre_grad = head_gelu_pull(back_dense(cot_low, head_fc2_weight))[0].astype(narrow_type)
    grad_head_fc1_weight = outer_sum(head_low, head_pre_grad) * leader
    grad_head_fc1_bias = jnp.sum(head_pre_grad.astype(wide_type), axis=0) * leader
    branch_part, grad_head_gain, grad_head_bias = head_norm_pull(
        back_dense(head_pre_grad, head_fc1_weight)
    )
    grad_head_gain = grad_head_gain * leader
    grad_head_bias = grad_head_bias * leader
    branch_grad = (pooled_cot + branch_part).astype(narrow_type)
    grad_pool_out_weight = outer_sum(pooled_low, branch_grad) * leader
    grad_pool_out_bias = jnp.sum(branch_grad.astype(wide_type), axis=0) * leader
    pooled_grad = back_dense(branch_grad, pool_out_weight).reshape(groups, HEADS, head_dim)
    pool_delta = jnp.sum(pooled_heads * pooled_grad, axis=-1)
    pool_shares = jnp.where(own_valid[:, None, :], jnp.exp(pool_scores - pool_log[..., None]), 0.0)
    share_grad = jnp.einsum("ghd,gbhd->ghb", pooled_grad, values_wide, precision=highest)
    score_grad = pool_shares * (share_grad - pool_delta[..., None])
    query_grad_pool = (
        jnp.einsum(
            "ghb,gbhd->hd", score_grad, pool_keys.astype(wide_type), precision=highest
        ).reshape(model_width)
        * 0.125
    )
    pool_key_grad = (
        jnp.einsum(
            "ghb,hd->gbhd",
            score_grad,
            pool_query.reshape(HEADS, head_dim).astype(wide_type),
            precision=highest,
        )
        * 0.125
    ).astype(narrow_type)
    pool_value_grad = jnp.einsum(
        "ghb,ghd->gbhd", pool_shares, pooled_grad, precision=highest
    ).astype(narrow_type)
    pool_kv_grad = jnp.concatenate(
        [
            pool_key_grad.reshape(row_count, model_width),
            pool_value_grad.reshape(row_count, model_width),
        ],
        axis=1,
    )
    grad_pool_kv_weight = outer_sum(final_low, pool_kv_grad)
    grad_pool_value_bias = jnp.sum(pool_kv_grad[:, model_width:].astype(wide_type), axis=0)
    grad_pool_query_weight = probe_vector.astype(wide_type)[:, None] * query_grad_pool[None, :]
    grad_probe_vector = jnp.dot(
        pool_query_weight.astype(wide_type), query_grad_pool, precision=highest
    )
    encoded_grad, grad_final_gain, grad_final_bias = final_pull(
        back_dense(pool_kv_grad, pool_kv_weight)
    )
    mlp_grad = encoded_grad.astype(narrow_type)
    grad_fc2_weight = outer_sum(hidden_act, mlp_grad)
    grad_fc2_bias = jnp.sum(mlp_grad.astype(wide_type), axis=0)
    hidden_grad = hidden_pull(back_dense(mlp_grad, fc2_weight))[0].astype(narrow_type)
    grad_fc1_weight = outer_sum(normed2_low, hidden_grad)
    grad_fc1_bias = jnp.sum(hidden_grad.astype(wide_type), axis=0)
    residual_part, grad_norm2_gain, grad_norm2_bias = norm2_pull(
        back_dense(hidden_grad, fc1_weight)
    )
    residual_grad = encoded_grad + residual_part
    attn_grad_low = residual_grad.astype(narrow_type)
    grad_attn_weight = outer_sum(attended_low, attn_grad_low)
    grad_attn_bias = jnp.sum(attn_grad_low.astype(wide_type), axis=0)
    attended_grad = (
        back_dense(attn_grad_low, attn_weight)
        .astype(narrow_type)
        .reshape(groups, block_rows, model_width)
    )

    def shares_again(query_rows, some_keys, valid_keys, log_rows):
        return jnp.exp(scores_of(query_rows, some_keys, valid_keys) - log_rows[:, :, None])

    def attend_back(inputs):
        query_rows, whole_keys, whole_values, valid_keys, log_rows, grad_rows = inputs
        shares = shares_again(query_rows, whole_keys, valid_keys, log_rows)
        shares_grad = jnp.einsum(
            "qhd,khd->hqk",
            split_heads(grad_rows),
            split_heads(whole_values),
            preferred_element_type=wide_type,
        )
        row_delta = jnp.sum(shares * shares_grad, axis=-1, keepdims=True)
        scores_grad = (shares * (shares_grad - row_delta)).astype(narrow_type)
        query_grad = (
            jnp.einsum(
                "hqk,khd->qhd",
                scores_grad,
                split_heads(whole_keys),
                preferred_element_type=wide_type,
            )
            * 0.125
        )
        key_term = (
            jnp.einsum(
                "hqk,qhd->khd",
                scores_grad,
                split_heads(query_rows),
                preferred_element_type=wide_type,
            )
            * 0.125
        )
        value_term = jnp.einsum(
            "hqk,qhd->khd",
            shares.astype(narrow_type),
            split_heads(grad_rows),
            preferred_element_type=wide_type,
        )
        return (
            query_grad.reshape(-1, model_width),
            key_term.reshape(-1, model_width),
            value_term.reshape(-1, model_width),
        )

    query_grad, key_terms, value_terms = lax.map(
        attend_back, (query_blocks, key_whole, value_whole, key_valid, log_sums, attended_grad)
    )
    key_grad, value_grad = (
        lax.psum_scatter(
            key_terms.astype(jnp.bfloat16), "seq", scatter_dimension=1, tiled=True
        ).astype(jnp.float32),
        lax.psum_scatter(
            value_terms.astype(jnp.bfloat16), "seq", scatter_dimension=1, tiled=True
        ).astype(jnp.float32),
    )
    qkv_grad = jnp.concatenate(
        [
            query_grad.reshape(row_count, model_width).astype(narrow_type),
            key_grad.reshape(row_count, model_width).astype(narrow_type),
            value_grad.reshape(row_count, model_width).astype(narrow_type),
        ],
        axis=1,
    )
    grad_qkv_weight = outer_sum(normed1_low, qkv_grad)
    grad_query_bias = jnp.sum(qkv_grad[:, :model_width].astype(wide_type), axis=0)
    grad_value_bias = jnp.sum(qkv_grad[:, 2 * model_width :].astype(wide_type), axis=0)
    flat_part, grad_norm1_gain, grad_norm1_bias = norm1_pull(back_dense(qkv_grad, qkv_weight))
    patch_grad = (residual_grad + flat_part).reshape(groups, block_rows, model_width)
    summed = (
        lax.psum_scatter(grad_norm1_gain, ("img", "seq"), scatter_dimension=0, tiled=True),
        lax.psum_scatter(grad_norm1_bias, ("img", "seq"), scatter_dimension=0, tiled=True),
        lax.psum_scatter(grad_qkv_weight, ("img", "seq"), scatter_dimension=0, tiled=True),
        lax.psum_scatter(grad_query_bias, ("img", "seq"), scatter_dimension=0, tiled=True),
        lax.psum_scatter(grad_value_bias, ("img", "seq"), scatter_dimension=0, tiled=True),
        lax.psum_scatter(grad_attn_weight, ("img", "seq"), scatter_dimension=0, tiled=True),
        lax.psum_scatter(grad_attn_bias, ("img", "seq"), scatter_dimension=0, tiled=True),
        lax.psum_scatter(grad_norm2_gain, ("img", "seq"), scatter_dimension=0, tiled=True),
        lax.psum_scatter(grad_norm2_bias, ("img", "seq"), scatter_dimension=0, tiled=True),
        lax.psum_scatter(grad_fc1_weight, ("img", "seq"), scatter_dimension=0, tiled=True),
        lax.psum_scatter(grad_fc1_bias, ("img", "seq"), scatter_dimension=0, tiled=True),
        lax.psum_scatter(grad_fc2_weight, ("img", "seq"), scatter_dimension=0, tiled=True),
        lax.psum_scatter(grad_fc2_bias, ("img", "seq"), scatter_dimension=0, tiled=True),
        lax.psum_scatter(grad_final_gain, ("img", "seq"), scatter_dimension=0, tiled=True),
        lax.psum_scatter(grad_final_bias, ("img", "seq"), scatter_dimension=0, tiled=True),
        lax.psum_scatter(grad_probe_vector, ("img", "seq"), scatter_dimension=0, tiled=True),
        lax.psum_scatter(grad_pool_query_weight, ("img", "seq"), scatter_dimension=0, tiled=True),
        lax.psum_scatter(query_grad_pool, ("img", "seq"), scatter_dimension=0, tiled=True),
        lax.psum_scatter(grad_pool_kv_weight, ("img", "seq"), scatter_dimension=0, tiled=True),
        lax.psum_scatter(grad_pool_value_bias, ("img", "seq"), scatter_dimension=0, tiled=True),
        lax.psum_scatter(grad_pool_out_weight, ("img", "seq"), scatter_dimension=0, tiled=True),
        lax.psum_scatter(grad_pool_out_bias, ("img", "seq"), scatter_dimension=0, tiled=True),
        lax.psum_scatter(grad_head_gain, ("img", "seq"), scatter_dimension=0, tiled=True),
        lax.psum_scatter(grad_head_bias, ("img", "seq"), scatter_dimension=0, tiled=True),
        lax.psum_scatter(grad_head_fc1_weight, ("img", "seq"), scatter_dimension=0, tiled=True),
        lax.psum_scatter(grad_head_fc1_bias, ("img", "seq"), scatter_dimension=0, tiled=True),
        lax.psum_scatter(grad_head_fc2_weight, ("img", "seq"), scatter_dimension=0, tiled=True),
        lax.psum_scatter(grad_head_fc2_bias, ("img", "seq"), scatter_dimension=0, tiled=True),
    )
    return (pooled, patch_grad, *summed)


def solution(mesh):
    in_specs = (
        P("img", "seq", None),
        P("img"),
        P("img", None),
        P(("img", "seq")),
        P(("img", "seq")),
        P(("img", "seq"), None),
        P(("img", "seq")),
        P(("img", "seq")),
        P(("img", "seq"), None),
        P(("img", "seq")),
        P(("img", "seq")),
        P(("img", "seq")),
        P(("img", "seq"), None),
        P(("img", "seq")),
        P(("img", "seq"), None),
        P(("img", "seq")),
        P(("img", "seq")),
        P(("img", "seq")),
        P(("img", "seq")),
        P(("img", "seq"), None),
        P(("img", "seq")),
        P(("img", "seq"), None),
        P(("img", "seq")),
        P(("img", "seq"), None),
        P(("img", "seq")),
        P(("img", "seq")),
        P(("img", "seq")),
        P(("img", "seq"), None),
        P(("img", "seq")),
        P(("img", "seq"), None),
        P(("img", "seq")),
    )
    out_specs = (
        P("img", None),
        P("img", "seq", None),
        P(("img", "seq")),
        P(("img", "seq")),
        P(("img", "seq"), None),
        P(("img", "seq")),
        P(("img", "seq")),
        P(("img", "seq"), None),
        P(("img", "seq")),
        P(("img", "seq")),
        P(("img", "seq")),
        P(("img", "seq"), None),
        P(("img", "seq")),
        P(("img", "seq"), None),
        P(("img", "seq")),
        P(("img", "seq")),
        P(("img", "seq")),
        P(("img", "seq")),
        P(("img", "seq"), None),
        P(("img", "seq")),
        P(("img", "seq"), None),
        P(("img", "seq")),
        P(("img", "seq"), None),
        P(("img", "seq")),
        P(("img", "seq")),
        P(("img", "seq")),
        P(("img", "seq"), None),
        P(("img", "seq")),
        P(("img", "seq"), None),
        P(("img", "seq")),
    )
    return jax.shard_map(local, mesh=mesh, in_specs=in_specs, out_specs=out_specs, check_vma=False)
```

profile of v0, /device:TPU:0, one launch (start us, length us, event | category | flops | bytes accessed | tf_op | source)
XLA Modules:
  0.0 2628.4 jit_solution(14361483030033666136)
XLA Ops:
  24.7 44.1 %all-reduce.39 = (bf16[768]{0:T(1024)(128)(2,1)S(1)}, bf16[768]{0:T(1024)(128)(2,1)S(1)}, bf16[768]{0:T(1024)(128)(2,1)S(1)}, bf16[768]{0:T(1024)(128)(2,1)S(1)}...) all-reduce(bf16[768]{0:T(1024)(128)(2,1)S(1)} %dynamic-update-slice, ...), channel_id=1, replica_groups=mesh['img'=16,'seq'=2] {'img','seq'}, use_global_device_ids=true, to_apply=%add | all-reduce | flops 19200 | bytes 76800
  136.1 75.2 %all-gather.21.cloned.1.call-done = bf16[4,1024,768]{1,2,0:T(8,128)(2,1)} async-done(((bf16[4,512,768]{1,2,0:T(8,128)(2,1)}), bf16[4,1024,768]{1,2,0:T(8,128)(2,1)}) %all-gather.21.cloned.1.call-update) | async-done | bytes 6291472 | tf_op jit(solution)/shard_map/all_gather | solution.py:190
  211.3 81.8 %all-gather.23.cloned.1.call-done = bf16[4,1024,768]{1,2,0:T(8,128)(2,1)} async-done(((bf16[4,512,768]{1,2,0:T(8,128)(2,1)}), bf16[4,1024,768]{1,2,0:T(8,128)(2,1)}) %all-gather.23.cloned.1.call-update) | async-done | bytes 6291472 | tf_op jit(solution)/shard_map/all_gather | solution.py:189
  295.0 152.1 %while.34 = (s32[]{:T(128)}, bf16[4,512,768]{2,1,0:T(8,128)(2,1)}, f32[4,12,512]{2,1,0:T(8,128)}, bf16[4,1024,768]{1,2,0:T(8,128)(2,1)}, pred[4,1024]{1,0:T(4,12...) while((s32[]{:T(128)}, bf16[4,512,768]{2,1,0:T(8,128)(2,1)}, ...), condition=%wide.region_5.6_spmd.clone, body=%wide.region_2.5_spmd.sunk.clone | while | flops 1686104064 | bytes 91437144 | solution.py:207
  457.7 24.4 multiply_convert_fusion.1
  501.3 38.8 %all-gather.31.cloned.1.call-done = bf16[768,1536]{1,0:T(8,128)(2,1)} async-done(((bf16[24,1536]{1,0:T(8,128)(2,1)}), bf16[768,1536]{1,0:T(8,128)(2,1)}) %all-gather.31.cloned.1.call-update) | async-done | bytes 2359312 | tf_op jit(solution)/shard_map/all_gather | solution.py:144
  597.9 63.5 %all-gather.35.cloned.1.call-done = bf16[768,3072]{1,0:T(8,128)(2,1)} async-done(((bf16[24,3072]{1,0:T(8,128)(2,1)}), bf16[768,3072]{1,0:T(8,128)(2,1)}) %all-gather.35.cloned.1.call-update) | async-done | bytes 4718608 | tf_op jit(solution)/shard_map/all_gather | solution.py:150
  664.6 62.3 %all-gather.37.cloned.1.call-done = bf16[3072,768]{1,0:T(8,128)(2,1)} async-done(((bf16[96,768]{1,0:T(8,128)(2,1)}), bf16[3072,768]{1,0:T(8,128)(2,1)}) %all-gather.37.cloned.1.call-update) | async-done | bytes 4718608 | tf_op jit(solution)/shard_map/all_gather | solution.py:152
  764.8 33.8 %convert_reduce_fusion = (f32[3072]{0:T(1024)}, bf16[2048,3072]{1,0:T(8,128)(2,1)}) fusion(f32[2048,3072]{1,0:T(8,128)} %get-tuple-element.372, f32[3072]{0:T(1024)S(1)} %copy-done.74, bf16[2048,768]{1,0:T(8,128)(2,1)} %get-tuple-element.338, bf16[3072,768]{1,0:T(8,128)(2,1)} %all-gather.29.cloned.1.call-done), kind=kOutput, calls=%fused_computation.42 | convolution fusion | flops 9808376832 | bytes 45637632 | tf_op jit(solution)/shard_map/dot_general | solution.py:47
  798.6 17.4 multiply_reduce_fusion.2
  827.9 351.0 %while.35 = (s32[]{:T(128)}, bf16[4,512,768]{2,1,0:T(8,128)(2,1)}, bf16[4,1024,768]{2,1,0:T(8,128)(2,1)}, bf16[4,1024,768]{2,1,0:T(8,128)(2,1)}, bf16[4,1024,768...) while((s32[]{:T(128)}, bf16[4,512,768]{2,1,0:T(8,128)(2,1)}, ...), condition=%wide.region_23.24_spmd.clone, body=%wide.region_21.23_spmd.sunk.clone | while | flops 4123256832 | bytes 277788800 | solution.py:380
  847.0 17.4 multiply_reduce_fusion.13
  864.4 16.7 multiply_convert_fusion.9
  934.6 17.4 multiply_reduce_fusion.13
  952.0 16.7 multiply_convert_fusion.9
  1022.3 17.4 multiply_reduce_fusion.13
  1039.7 16.7 multiply_convert_fusion.9
  1109.8 17.4 multiply_reduce_fusion.13
  1127.2 16.7 multiply_convert_fusion.9
  1195.4 59.6 %reduce-scatter.12.cloned.1.call-done = bf16[4,512,768]{2,1,0:T(8,128)(2,1)} async-done(((bf16[4,1024,768]{2,1,0:T(8,128)(2,1)}), bf16[4,512,768]{2,1,0:T(8,128)(2,1)}) %reduce-scatter.12.cloned.1.call-update) | async-done | bytes 3145744 | tf_op jit(solution)/shard_map/reduce_scatter | solution.py:384
  1255.0 79.5 %reduce-scatter.14.cloned.1.call-done = bf16[4,512,768]{2,1,0:T(8,128)(2,1)} async-done(((bf16[4,1024,768]{2,1,0:T(8,128)(2,1)}), bf16[4,512,768]{2,1,0:T(8,128)(2,1)}) %reduce-scatter.14.cloned.1.call-update) | async-done | bytes 3145744 | tf_op jit(solution)/shard_map/reduce_scatter | solution.py:387
  1397.8 18.2 fusion.85
  1448.8 54.3 %all-reduce.42.cloned.1.call-done = (f32[768]{0:T(1024)}, f32[768]{0:T(1024)}, f32[768]{0:T(1024)}, f32[768]{0:T(1024)}, f32[768]{0:T(1024)}, /*index=5*/f32[768...) async-done(((f32[768]{0:T(1024)}, f32[768]{0:T(1024)}, ...) | async-done | bytes 76816
  1527.1 82.4 %reduce-scatter.28.cloned.1.call-done = f32[24,768]{1,0:T(8,128)} async-done(((f32[768,768]{1,0:T(8,128)}), f32[24,768]{1,0:T(8,128)}) %reduce-scatter.28.cloned.1.call-update) | async-done | bytes 73744 | tf_op jit(solution)/shard_map/reduce_scatter | solution.py:425
  1609.5 104.6 %reduce-scatter.18.cloned.1.call-done = f32[24,768]{1,0:T(8,128)} async-done(((f32[768,768]{1,0:T(8,128)}), f32[24,768]{1,0:T(8,128)}) %reduce-scatter.18.cloned.1.call-update) | async-done | bytes 73744 | tf_op jit(solution)/shard_map/reduce_scatter | solution.py:410
  1714.1 103.8 %reduce-scatter.24.cloned.1.call-done = f32[24,768]{1,0:T(8,128)} async-done(((f32[768,768]{1,0:T(8,128)}), f32[24,768]{1,0:T(8,128)}) %reduce-scatter.24.cloned.1.call-update) | async-done | bytes 73744 | tf_op jit(solution)/shard_map/reduce_scatter | solution.py:421
  1818.0 112.8 %reduce-scatter.26.cloned.1.call-done = f32[24,1536]{1,0:T(8,128)} async-done(((f32[768,1536]{1,0:T(8,128)}), f32[24,1536]{1,0:T(8,128)}) %reduce-scatter.26.cloned.1.call-update) | async-done | bytes 147472 | tf_op jit(solution)/shard_map/reduce_scatter | solution.py:423
  1930.8 141.2 %reduce-scatter.30.cloned.1.call-done = f32[24,3072]{1,0:T(8,128)} async-done(((f32[768,3072]{1,0:T(8,128)}), f32[24,3072]{1,0:T(8,128)}) %reduce-scatter.30.cloned.1.call-update) | async-done | bytes 294928 | tf_op jit(solution)/shard_map/reduce_scatter | solution.py:429
  2072.0 141.8 %reduce-scatter.22.cloned.1.call-done = f32[96,768]{1,0:T(8,128)} async-done(((f32[3072,768]{1,0:T(8,128)}), f32[96,768]{1,0:T(8,128)}) %reduce-scatter.22.cloned.1.call-update) | async-done | bytes 294928 | tf_op jit(solution)/shard_map/reduce_scatter | solution.py:416
  2213.8 141.3 %reduce-scatter.20.cloned.1.call-done = f32[24,3072]{1,0:T(8,128)} async-done(((f32[768,3072]{1,0:T(8,128)}), f32[24,3072]{1,0:T(8,128)}) %reduce-scatter.20.cloned.1.call-update) | async-done | bytes 294928 | tf_op jit(solution)/shard_map/reduce_scatter | solution.py:414
  2355.1 142.2 %reduce-scatter.32.cloned.1.call-done = f32[96,768]{1,0:T(8,128)} async-done(((f32[3072,768]{1,0:T(8,128)}), f32[96,768]{1,0:T(8,128)}) %reduce-scatter.32.cloned.1.call-update) | async-done | bytes 294928 | tf_op jit(solution)/shard_map/reduce_scatter | solution.py:431
  2497.4 124.3 %reduce-scatter.16.cloned.1.call-done = f32[24,2304]{1,0:T(8,128)} async-done(((f32[768,2304]{1,0:T(8,128)}), f32[24,2304]{1,0:T(8,128)}) %reduce-scatter.16.cloned.1.call-update) | async-done | bytes 221200 | tf_op jit(solution)/shard_map/reduce_scatter | solution.py:407
  (532 shorter events, 728.0 us)
Async XLA Ops:
  7.2 70.7 %all-gather.19.cloned.1.call-start = ((), (), s32[]{:S(2)}) async-start(), calls=%async_computation.12 | async-start | bytes 3649536 | tf_op jit(solution)/shard_map/all_gather | solution.py:128
  7.9 122.4 %all-gather.17.cloned.1.call-start = ((), (), s32[]{:S(2)}) async-start(), calls=%async_computation.11 | async-start | bytes 1216512 | tf_op jit(solution)/shard_map/all_gather | solution.py:142
  8.7 202.6 %all-gather.21.cloned.1.call-start = ((), (), s32[]{:S(2)}) async-start(), calls=%async_computation.13 | async-start | bytes 9437184 | tf_op jit(solution)/shard_map/all_gather | solution.py:190
  98.9 194.3 %all-gather.23.cloned.1.call-start = ((), (), s32[]{:S(2)}) async-start(), calls=%async_computation.14 | async-start | bytes 9437184 | tf_op jit(solution)/shard_map/all_gather | solution.py:189
  104.9 342.1 %all-gather.25.cloned.1.call-start = ((), (), s32[]{:S(2)}) async-start(), calls=%async_computation.15 | async-start | bytes 1216512 | tf_op jit(solution)/shard_map/all_gather | solution.py:131
  105.5 352.1 %all-gather.27.cloned.1.call-start = ((), (), s32[]{:S(2)}) async-start(), calls=%async_computation.16 | async-start | bytes 4866048 | tf_op jit(solution)/shard_map/all_gather | solution.py:135
  106.1 376.0 %all-gather.29.cloned.1.call-start = ((), (), s32[]{:S(2)}) async-start(), calls=%async_computation.17 | async-start | bytes 4866048 | tf_op jit(solution)/shard_map/all_gather | solution.py:137
  106.9 433.2 %all-gather.31.cloned.1.call-start = ((), (), s32[]{:S(2)}) async-start(), calls=%async_computation.18 | async-start | bytes 2433024 | tf_op jit(solution)/shard_map/all_gather | solution.py:144
  107.6 488.4 %all-gather.33.cloned.1.call-start = ((), (), s32[]{:S(2)}) async-start(), calls=%async_computation.19 | async-start | bytes 1216512 | tf_op jit(solution)/shard_map/all_gather | solution.py:146
  108.3 553.1 %all-gather.35.cloned.1.call-start = ((), (), s32[]{:S(2)}) async-start(), calls=%async_computation.20 | async-start | bytes 4866048 | tf_op jit(solution)/shard_map/all_gather | solution.py:150
  108.9 618.0 %all-gather.37.cloned.1.call-start = ((), (), s32[]{:S(2)}) async-start(), calls=%async_computation.21 | async-start | bytes 4866048 | tf_op jit(solution)/shard_map/all_gather | solution.py:152
  109.7 1145.3 %reduce-scatter.12.cloned.1.call-start = ((), (), s32[]{:S(2)}) async-start(), calls=%async_computation.22 | async-start | bytes 9437184 | tf_op jit(solution)/shard_map/reduce_scatter | solution.py:384
  453.5 362.5 %copy-start.36 = (f32[2048]{0:T(1024)}, f32[2048]{0:T(1024)S(1)}, u32[]{:S(2)}) copy-start(f32[2048]{0:T(1024)S(1)} %broadcast_multiply_fusion.3) | copy-start | bytes 24580
  457.6 358.4 %copy-start.54 = (f32[2048]{0:T(1024)}, f32[2048]{0:T(1024)S(1)}, u32[]{:S(2)}) copy-start(f32[2048]{0:T(1024)S(1)} %fusion.65) | copy-start | bytes 24580
  497.7 261.3 %copy-start.38 = (f32[2048]{0:T(1024)}, f32[2048]{0:T(1024)S(1)}, u32[]{:S(2)}) copy-start(f32[2048]{0:T(1024)S(1)} %broadcast_multiply_fusion.2) | copy-start | bytes 24580
  501.3 257.8 %copy-start.56 = (f32[2048]{0:T(1024)}, f32[2048]{0:T(1024)S(1)}, u32[]{:S(2)}) copy-start(f32[2048]{0:T(1024)S(1)} %fusion.66) | copy-start | bytes 24580
  573.3 153.6 %copy-start.34 = (f32[4,768]{1,0:T(4,128)S(1)}, f32[4,768]{1,0:T(4,128)}, u32[]{:S(2)}) copy-start(f32[4,768]{1,0:T(4,128)} %param.37) | copy-start | bytes 36868
  1179.0 155.5 %reduce-scatter.14.cloned.1.call-start = ((), (), s32[]{:S(2)}) async-start(), calls=%async_computation.23 | async-start | bytes 9437184 | tf_op jit(solution)/shard_map/reduce_scatter | solution.py:387
  1179.8 154.7 %copy-start.2 = (bf16[4,512,768]{2,1,0:T(8,128)(2,1)S(1)}, bf16[4,512,768]{2,1,0:T(8,128)(2,1)}, u32[]{:S(2)}) copy-start(bf16[4,512,768]{2,1,0:T(8,128)(2,1)} %param.35) | copy-start | bytes 9437188
  1179.8 154.7 %copy-start.33 = (f32[1,4,4,128]{3,1,2,0:T(4,128)S(1)}, f32[1,4,4,128]{3,1,2,0:T(4,128)}, u32[]{:S(2)}) copy-start(f32[1,4,4,128]{3,1,2,0:T(4,128)} %copy-done.32) | copy-start | bytes 24580
  1179.8 154.7 %copy-start.46 = (f32[768]{0:T(1024)S(1)}, f32[768]{0:T(1024)}, u32[]{:S(2)}) copy-start(f32[768]{0:T(1024)} %copy-done.45) | copy-start | bytes 9220
  1184.7 161.9 %copy-start.53 = (f32[768]{0:T(1024)}, f32[768]{0:T(1024)S(1)}, u32[]{:S(2)}) copy-start(f32[768]{0:T(1024)S(1)} %mul.571) | copy-start | bytes 9220
  1195.4 307.7 %all-reduce.42.cloned.1.call-start = ((), (), s32[]{:S(2)}) async-start(), calls=%async_computation.33 | async-start | bytes 188416
  1351.8 257.7 %reduce-scatter.28.cloned.1.call-start = ((), (), s32[]{:S(2)}) async-start(), calls=%async_computation.30 | async-start | bytes 2433024 | tf_op jit(solution)/shard_map/reduce_scatter | solution.py:425
  1353.9 360.2 %reduce-scatter.18.cloned.1.call-start = ((), (), s32[]{:S(2)}) async-start(), calls=%async_computation.25 | async-start | bytes 2433024 | tf_op jit(solution)/shard_map/reduce_scatter | solution.py:410
  1361.8 456.1 %reduce-scatter.24.cloned.1.call-start = ((), (), s32[]{:S(2)}) async-start(), calls=%async_computation.28 | async-start | bytes 2433024 | tf_op jit(solution)/shard_map/reduce_scatter | solution.py:421
  1362.5 568.3 %reduce-scatter.26.cloned.1.call-start = ((), (), s32[]{:S(2)}) async-start(), calls=%async_computation.29 | async-start | bytes 4866048 | tf_op jit(solution)/shard_map/reduce_scatter | solution.py:423
  1375.1 696.8 %reduce-scatter.30.cloned.1.call-start = ((), (), s32[]{:S(2)}) async-start(), calls=%async_computation.31 | async-start | bytes 9732096 | tf_op jit(solution)/shard_map/reduce_scatter | solution.py:429
  1380.4 833.4 %reduce-scatter.22.cloned.1.call-start = ((), (), s32[]{:S(2)}) async-start(), calls=%async_computation.27 | async-start | bytes 9732096 | tf_op jit(solution)/shard_map/reduce_scatter | solution.py:416
  1397.1 958.0 %reduce-scatter.20.cloned.1.call-start = ((), (), s32[]{:S(2)}) async-start(), calls=%async_computation.26 | async-start | bytes 9732096 | tf_op jit(solution)/shard_map/reduce_scatter | solution.py:414
  1416.0 1081.4 %reduce-scatter.32.cloned.1.call-start = ((), (), s32[]{:S(2)}) async-start(), calls=%async_computation.32 | async-start | bytes 9732096 | tf_op jit(solution)/shard_map/reduce_scatter | solution.py:431
  1421.9 1199.8 %reduce-scatter.16.cloned.1.call-start = ((), (), s32[]{:S(2)}) async-start(), calls=%async_computation.24 | async-start | bytes 7299072 | tf_op jit(solution)/shard_map/reduce_scatter | solution.py:407
  (85 other events, 1803.2 us)
Sparse Core Ops, SparseCore 0:
  11.0 63.2 all-gather.18
  77.1 53.2 all-gather.16
  131.9 79.3 all-gather.20
  212.7 80.3 all-gather.22
  295.9 54.1 all-gather.24
  352.9 62.5 all-gather.26
  418.4 62.4 all-gather.28
  483.9 56.1 all-gather.30
  543.0 52.9 all-gather.32
  598.8 62.6 all-gather.34
  664.4 62.4 all-gather.36
  1179.1 75.8 reduce-scatter.11
  1257.4 77.0 reduce-scatter.13
  1352.0 151.0 all-reduce.41
  1508.8 100.6 reduce-scatter.27
  1616.1 98.0 reduce-scatter.17
  1719.8 98.0 reduce-scatter.23
  1824.8 105.9 reduce-scatter.25
  1937.3 134.6 reduce-scatter.29
  2079.3 134.4 reduce-scatter.21
  2220.3 134.7 reduce-scatter.19
  2362.6 134.7 reduce-scatter.31
  2503.6 118.0 reduce-scatter.15
where the time goes:
time: 2640 us; the launch traced here: 2630 us
  waiting for transfers between devices  1630 us (62%)
  matrix products  553 us (21%)
  local copies, waits for them, and re-layouts  193 us (7%)
  other arithmetic  175 us (7%)
  blocking collectives  57.3 us (2%)
    reduce_scatter x1, waiting for transfers between devices, local(): lax.psum_scatter(grad_head_fc2_weight, ('img', 'seq'), scatter_dimension=...  142 us
    reduce_scatter x1, waiting for transfers between devices, local(): lax.psum_scatter(grad_fc2_weight, ('img', 'seq'), scatter_dimension=0, ti...  142 us
    reduce_scatter x1, waiting for transfers between devices, local(): lax.psum_scatter(grad_fc1_weight, ('img', 'seq'), scatter_dimension=0, ti...  141 us
    reduce_scatter x1, waiting for transfers between devices, local(): lax.psum_scatter(grad_head_fc1_weight, ('img', 'seq'), scatter_dimension=...  141 us
    reduce_scatter x1, waiting for transfers between devices, local(): lax.psum_scatter(grad_qkv_weight, ('img', 'seq'), scatter_dimension=0, ti...  124 us
    reduce_scatter x1, waiting for transfers between devices, local(): lax.psum_scatter(grad_pool_kv_weight, ('img', 'seq'), scatter_dimension=0...  113 us
    reduce_scatter x1, waiting for transfers between devices, local(): lax.psum_scatter(grad_attn_weight, ('img', 'seq'), scatter_dimension=0, t...  105 us
    reduce_scatter x1, waiting for transfers between devices, local(): lax.psum_scatter(grad_pool_query_weight, ('img', 'seq'), scatter_dimensio...  104 us
  transfers between devices with their start and end apart: 23, of which 19 were waited for; matrix products, arithmetic and copies ran while one was open for 16% of the time, Pallas kernels for 0%

commit v1 on v0

v1 whole, which is shorter than its diff:
```python
import functools

import jax
import jax.numpy as jnp
from jax import lax
from jax.experimental import pallas as pl
from jax.experimental.pallas import tpu as pltpu
from jax.sharding import PartitionSpec as P

HEADS = 12
HEAD_DIM = 64
BLOCK = 256
PAIR = 128
wide = jnp.float32
low = jnp.bfloat16
masked_score = -1e30
norm_epsilon = 1e-06
root_two_pi = 0.7978845608028654
vmem_bytes = 60 * 1024 * 1024


def dot_nn(a, b):
    return jnp.dot(a, b, preferred_element_type=wide)


def dot_nt(a, b):
    return lax.dot_general(a, b, (((1,), (1,)), ((), ())), preferred_element_type=wide)


def dot_tn(a, b):
    return lax.dot_general(a, b, (((0,), (0,)), ((), ())), preferred_element_type=wide)


def halves(v):
    top = v.astype(low)
    return top, (v - top.astype(wide)).astype(low)


def normalise(v):
    centred = v - jnp.mean(v, axis=-1, keepdims=True)
    spread = jnp.mean(centred * centred, axis=-1, keepdims=True)
    scale = lax.rsqrt(spread + norm_epsilon)
    return centred * scale, scale


def norm_back(grad, gain, normal, scale):
    gn = grad * gain
    return (
        gn
        - jnp.mean(gn, axis=-1, keepdims=True)
        - normal * jnp.mean(gn * normal, axis=-1, keepdims=True)
    ) * scale


def column_sum(v):
    return jnp.sum(v, axis=0, keepdims=True)


def params(rank):
    return pltpu.CompilerParams(
        dimension_semantics=("arbitrary",) * rank, vmem_limit_bytes=vmem_bytes
    )


def whole(shape):
    return pl.BlockSpec(
        shape, lambda *_: (0,) * len(shape), pipeline_mode=pl.Buffered(1)
    )


def cost(flops, nbytes, exps=0):
    return pl.CostEstimate(flops=int(flops), bytes_accessed=int(nbytes), transcendentals=int(exps))


class Sizes:
    def __init__(self, images, length, width, hidden):
        self.images, self.length, self.width, self.hidden = images, length, width, hidden
        self.rows = images * length
        self.blocks = length // BLOCK
        self.pairs = width // PAIR

    def row_spec(self, cols):
        blocks = self.blocks

        def index(i, b, meta):
            return i * blocks + jnp.clip(b, 0, jnp.maximum(meta[i] - 1, 0)), 0

        return pl.BlockSpec((BLOCK, cols), index)

    def lane_spec(self, rows):
        def index(i, b, meta):
            return i, 0, jnp.clip(b, 0, jnp.maximum(meta[i] - 1, 0))

        return pl.BlockSpec((1, rows, BLOCK), index)

    def image_spec(self, rows, cols):
        return pl.BlockSpec((1, rows, cols), lambda i, b, meta: (i, 0, 0))


(
    NORM1_GAIN,
    NORM1_BIAS,
    QUERY_BIAS,
    VALUE_BIAS,
    ATTN_BIAS,
    NORM2_GAIN,
    NORM2_BIAS,
    FC2_BIAS,
    FINAL_GAIN,
    FINAL_BIAS,
    POOL_QUERY_BIAS,
    POOL_VALUE_BIAS,
    POOL_OUT_BIAS,
    HEAD_GAIN,
    HEAD_BIAS,
    HEAD_FC2_BIAS,
) = range(16)


def row_of(ref, at):
    return ref[at : at + 1, :]


def qkv_body(meta, x, vec, weight, qkv, normed):
    @pl.when(pl.program_id(1) < meta[pl.program_id(0)])
    def _():
        width = x.shape[1]
        normal, _ = normalise(x[...].astype(wide))
        rows = (normal * row_of(vec, NORM1_GAIN) + row_of(vec, NORM1_BIAS)).astype(low)
        normed[...] = rows
        for part, bias in enumerate((QUERY_BIAS, None, VALUE_BIAS)):
            cols = slice(part * width, (part + 1) * width)
            out = dot_nn(rows, weight[:, cols])
            if bias is not None:
                out = out + row_of(vec, bias)
            qkv[:, cols] = out.astype(low)


def qkv_call(sz, meta, x, vec, weight):
    w = sz.width
    return pl.pallas_call(
        qkv_body,
        grid_spec=pltpu.PrefetchScalarGridSpec(
            num_scalar_prefetch=1,
            grid=(sz.images, sz.blocks),
            in_specs=[sz.row_spec(w), whole(vec.shape), whole(weight.shape)],
            out_specs=[sz.row_spec(3 * w), sz.row_spec(w)],
        ),
        out_shape=[
            jax.ShapeDtypeStruct((sz.rows, 3 * w), low),
            jax.ShapeDtypeStruct((sz.rows, w), low),
        ],
        compiler_params=params(2),
        cost_estimate=cost(6 * sz.rows * w * w, sz.rows * w * 10 + 6 * w * w),
        name="qkv",
    )(meta, x, vec, weight)


def attend_body(images, blocks, meta, q_ref, k_ref, v_ref, out_ref, lse_ref):
    at = pl.program_id(0)
    count, length = meta[at], meta[images + at]
    lane = lax.broadcasted_iota(jnp.int32, (BLOCK, PAIR), 1)
    first = lane < HEAD_DIM

    def variant(keys_in):
        near = keys_in - BLOCK
        column = lax.broadcasted_iota(jnp.int32, (BLOCK, BLOCK), 1) + near

        @pl.loop(0, count)
        def _(step):
            rows = pl.ds(pl.multiple_of(step * BLOCK, BLOCK), BLOCK)
            q = q_ref[rows, :]
            outs, logs = [], []
            for head in range(2):
                own = first if head == 0 else jnp.logical_not(first)
                qh = jnp.where(own, q, jnp.zeros_like(q))
                last = dot_nt(qh, k_ref[near:keys_in, :]) * 0.125
                last = jnp.where(column < length, last, masked_score)
                top = jnp.max(last, axis=1, keepdims=True)
                if near:
                    body = dot_nt(qh, k_ref[:near, :]) * 0.125
                    top = jnp.maximum(top, jnp.max(body, axis=1, keepdims=True))
                p_last = jnp.exp(last - top)
                total = jnp.sum(p_last, axis=1, keepdims=True)
                acc = dot_nn(p_last.astype(low), v_ref[near:keys_in, :])
                if near:
                    p_body = jnp.exp(body - top)
                    total = total + jnp.sum(p_body, axis=1, keepdims=True)
                    acc = acc + dot_nn(p_body.astype(low), v_ref[:near, :])
                outs.append(acc / total)
                logs.append(top + jnp.log(total))
            out_ref[rows, :] = jnp.where(first, outs[0], outs[1]).astype(low)
            both = jnp.where(lane == 0, logs[0], logs[1])
            lse_ref[0, :, rows] = both.T[:8, :]

    for keys in range(1, blocks + 1):
        pl.when(count == keys)(functools.partial(variant, keys * BLOCK))


def attend_call(sz, meta, qkv):
    pairs = sz.pairs

    def spec(part):
        return pl.BlockSpec((sz.length, PAIR), lambda i, p, m: (i, part * pairs + p))

    return pl.pallas_call(
        functools.partial(attend_body, sz.images, sz.blocks),
        grid_spec=pltpu.PrefetchScalarGridSpec(
            num_scalar_prefetch=1,
            grid=(sz.images, pairs),
            in_specs=[spec(0), spec(1), spec(2)],
            out_specs=[
                pl.BlockSpec((sz.length, PAIR), lambda i, p, m: (i, p)),
                pl.BlockSpec((1, 8, sz.length), lambda i, p, m: (i, p, 0)),
            ],
        ),
        out_shape=[
            jax.ShapeDtypeStruct((sz.rows, sz.width), low),
            jax.ShapeDtypeStruct((sz.images, 8 * pairs, sz.length), wide),
        ],
        compiler_params=params(2),
        cost_estimate=cost(
            4 * sz.rows * sz.length * sz.width,
            8 * sz.rows * sz.width,
            sz.rows * sz.length * HEADS,
        ),
        name="attend",
    )(meta, qkv, qkv, qkv)


def mlp_body(meta, x, att, vec, fcb, attn_w, fc1, fc2, res, n2, slope, act, enc, fin):
    @pl.when(pl.program_id(1) < meta[pl.program_id(0)])
    def _():
        width = x.shape[1]
        branch = dot_nn(att[...], attn_w[...]) + row_of(vec, ATTN_BIAS)
        rows = x[...].astype(wide) + branch
        res[...] = rows
        normal, _ = normalise(rows)
        normed = (normal * row_of(vec, NORM2_GAIN) + row_of(vec, NORM2_BIAS)).astype(low)
        n2[...] = normed
        total = rows + row_of(vec, FC2_BIAS)
        for part in range(fc1.shape[1] // width):
            cols = slice(part * width, (part + 1) * width)
            u = dot_nn(normed, fc1[:, cols]) + fcb[0:1, cols]
            square = u * u
            bend = jnp.tanh(root_two_pi * u * (1.0 + 0.044715 * square))
            half = 0.5 * (1.0 + bend)
            hidden = (u * half).astype(low)
            slope[:, cols] = (
                half
                + (0.5 * root_two_pi) * u * (1.0 - bend * bend) * (1.0 + 0.134145 * square)
            ).astype(low)
            act[:, cols] = hidden
            total = total + dot_nn(hidden, fc2[cols, :])
        enc[...] = total
        normal, _ = normalise(total)
        fin[...] = (normal * row_of(vec, FINAL_GAIN) + row_of(vec, FINAL_BIAS)).astype(low)


def mlp_call(sz, meta, x, att, vec, fcb, attn_w, fc1, fc2):
    w, f = sz.width, sz.hidden
    return pl.pallas_call(
        mlp_body,
        grid_spec=pltpu.PrefetchScalarGridSpec(
            num_scalar_prefetch=1,
            grid=(sz.images, sz.blocks),
            in_specs=[sz.row_spec(w), sz.row_spec(w)]
            + [whole(v.shape) for v in (vec, fcb, attn_w, fc1, fc2)],
            out_specs=[sz.row_spec(c) for c in (w, w, f, f, w, w)],
        ),
        out_shape=[
            jax.ShapeDtypeStruct((sz.rows, w), wide),
            jax.ShapeDtypeStruct((sz.rows, w), low),
            jax.ShapeDtypeStruct((sz.rows, f), low),
            jax.ShapeDtypeStruct((sz.rows, f), low),
            jax.ShapeDtypeStruct((sz.rows, w), wide),
            jax.ShapeDtypeStruct((sz.rows, w), low),
        ],
        compiler_params=params(2),
        cost_estimate=cost(
            sz.rows * w * (2 * w + 4 * f), sz.rows * (14 * w + 4 * f) + 4 * w * f, sz.rows * f
        ),
        name="mlp",
    )(meta, x, att, vec, fcb, attn_w, fc1, fc2)


HEAD_ROWS = 16


def head_body(
    images, blocks, meta, fin, probe_w, cot_ref, vec, fcb, pool_v, pool_out, fc1, fc2,
    pooled_ref, shares, lift, drop, outer, wide_rows, narrow_rows, sums, score,
):
    width, hidden = pool_out.shape[0], fc1.shape[1]
    head_row = lax.broadcasted_iota(jnp.int32, (HEAD_ROWS, width), 0)
    head_col = lax.broadcasted_iota(jnp.int32, (HEAD_ROWS, width), 1) // HEAD_DIM
    own = head_row == head_col
    row_id = lax.broadcasted_iota(jnp.int32, (HEAD_ROWS, 1), 0)
    probe_top, probe_rest = halves(probe_w[...])
    pooled_heads = jnp.zeros((HEAD_ROWS, width), wide)
    for i in range(images):
        count, length = meta[i], meta[images + i]
        base = i * blocks * BLOCK
        for b in range(blocks):
            cols = slice(b * BLOCK, (b + 1) * BLOCK)
            score[:, cols] = jnp.full((HEAD_ROWS, BLOCK), masked_score, wide)

            @pl.when(b < count)
            def _(b=b, cols=cols, base=base, length=length):
                rows = fin[base + b * BLOCK : base + (b + 1) * BLOCK, :]
                value = dot_nt(probe_top, rows) + dot_nt(probe_rest, rows)
                column = lax.broadcasted_iota(jnp.int32, (HEAD_ROWS, BLOCK), 1) + b * BLOCK
                score[:, cols] = jnp.where(column < length, value, masked_score)

        raised = jnp.exp(score[...] - jnp.max(score[...], axis=1, keepdims=True))
        share = raised / jnp.sum(raised, axis=1, keepdims=True)
        shares[i] = share
        lift[i] = jnp.zeros((HEAD_ROWS, width), wide)
        for b in range(blocks):
            cols = slice(b * BLOCK, (b + 1) * BLOCK)

            @pl.when(b < count)
            def _(b=b, cols=cols, base=base, i=i):
                rows = fin[base + b * BLOCK : base + (b + 1) * BLOCK, :]
                top, rest = halves(shares[i, :, cols])
                lift[i] += dot_nn(top, rows) + dot_nn(rest, rows)

        mixed = lift[i]
        outer[i] = mixed.astype(low)
        top, rest = halves(mixed)
        heads = dot_nn(top, pool_v[...]) + dot_nn(rest, pool_v[...])
        row = column_sum(jnp.where(own, heads, 0.0)) + row_of(vec, POOL_VALUE_BIAS)
        pooled_heads = jnp.where(row_id == i, row, pooled_heads)
    real = row_id < jnp.where(meta[0] > 0, images, 0)
    cot = jnp.where(real, cot_ref[...], 0.0)
    pooled_low = pooled_heads.astype(low)
    branch = dot_nn(pooled_low, pool_out[...]) + row_of(vec, POOL_OUT_BIAS)
    normal, scale = normalise(branch)
    gain = row_of(vec, HEAD_GAIN)
    normed = (normal * gain + row_of(vec, HEAD_BIAS)).astype(low)
    cot_low = cot.astype(low)
    total = branch + row_of(vec, HEAD_FC2_BIAS)
    back = jnp.zeros((HEAD_ROWS, width), wide)
    for part in range(hidden // width):
        cols = slice(part * width, (part + 1) * width)
        u = dot_nn(normed, fc1[:, cols]) + fcb[1:2, cols]
        square = u * u
        bend = jnp.tanh(root_two_pi * u * (1.0 + 0.044715 * square))
        half = 0.5 * (1.0 + bend)
        act = (u * half).astype(low)
        slope = half + (0.5 * root_two_pi) * u * (1.0 - bend * bend) * (1.0 + 0.134145 * square)
        total = total + dot_nn(act, fc2[cols, :])
        grad = jnp.where(real, dot_nt(cot_low, fc2[cols, :]) * slope, 0.0).astype(low)
        back = back + dot_nt(grad, fc1[:, cols])
        narrow_rows[:, cols] = act
        wide_rows[:, cols] = grad
    pooled_ref[...] = total
    sums[0:1, :] = column_sum(jnp.where(real, back * normal, 0.0))
    sums[1:2, :] = column_sum(jnp.where(real, back, 0.0))
    branch_grad = jnp.where(real, cot + norm_back(back, gain, normal, scale), 0.0).astype(low)
    pooled_grad = dot_nt(branch_grad, pool_out[...])
    narrow_rows[:, hidden : hidden + width] = normed
    narrow_rows[:, hidden + width : hidden + 2 * width] = pooled_low
    wide_rows[:, hidden : hidden + width] = branch_grad
    wide_rows[:, hidden + width : hidden + 2 * width] = pooled_grad.astype(low)
    wide_rows[:, hidden + 2 * width : hidden + 3 * width] = cot_low
    for i in range(images):
        spread = jnp.where(own, pooled_grad[i : i + 1, :], 0.0)
        top, rest = halves(spread)
        raised = dot_nt(top, pool_v[...]) + dot_nt(rest, pool_v[...])
        both = jnp.sum(raised * lift[i], axis=1, keepdims=True)
        drop[i] = jnp.broadcast_to(both, (HEAD_ROWS, PAIR))
        lift[i] = raised


def head_call(sz, meta, fin, probe_w, cot, vec, fcb, pool_v, pool_out, fc1, fc2):
    w, f, n = sz.width, sz.hidden, sz.images

    def out(shape, dtype):
        return jax.ShapeDtypeStruct(shape, dtype)

    shapes = [
        out((HEAD_ROWS, w), wide),
        out((n, HEAD_ROWS, sz.length), wide),
        out((n, HEAD_ROWS, w), wide),
        out((n, HEAD_ROWS, PAIR), wide),
        out((n, HEAD_ROWS, w), low),
        out((HEAD_ROWS, f + 3 * w), low),
        out((HEAD_ROWS, f + 2 * w), low),
        out((8, w), wide),
    ]
    ins = (fin, probe_w, cot, vec, fcb, pool_v, pool_out, fc1, fc2)
    return pl.pallas_call(
        functools.partial(head_body, sz.images, sz.blocks),
        grid_spec=pltpu.PrefetchScalarGridSpec(
            num_scalar_prefetch=1,
            grid=(1,),
            in_specs=[whole(v.shape) for v in ins],
            out_specs=[pl.BlockSpec(s.shape, lambda *_, r=len(s.shape): (0,) * r) for s in shapes],
            scratch_shapes=[pltpu.VMEM((HEAD_ROWS, sz.length), wide)],
        ),
        out_shape=shapes,
        compiler_params=params(1),
        cost_estimate=cost(16 * 8 * w * f, sz.rows * w * 2 + 4 * w * f + 4 * w * w),
        name="head",
    )(meta, *ins)


def back_body(
    meta, fin, enc, res, att, slope, shares, lift, drop, probe_w, spread, vec, attn_w, fc1, fc2,
    g_mlp, g_hidden, g_res, g_branch, g_att, delta, mix, sums, fc1_sum,
):
    @pl.when((pl.program_id(0) == 0) & (pl.program_id(1) == 0))
    def _():
        mix[...] = jnp.zeros_like(mix)
        sums[...] = jnp.zeros_like(sums)
        fc1_sum[...] = jnp.zeros_like(fc1_sum)

    @pl.when(pl.program_id(1) < meta[pl.program_id(0)])
    def _():
        width = fin.shape[1]
        rows = fin[...]
        share = shares[0]
        lift_top, lift_rest = halves(lift[0])
        probe_top, probe_rest = halves(probe_w[...])
        reach = dot_nt(lift_top, rows) + dot_nt(lift_rest, rows)
        g_score = share * (reach - drop[0][:, :1])
        top, rest = halves(g_score)
        mix[...] += dot_nn(top, rows) + dot_nn(rest, rows)
        share_top, share_rest = halves(share)
        left = jnp.concatenate([top, share_top, rest, share_rest, top, share_top], axis=0)
        right = jnp.concatenate(
            [probe_top, lift_top, probe_top, lift_top, probe_rest, lift_rest], axis=0
        )
        g_fin = dot_tn(left, right)
        normal, scale = normalise(enc[...])
        sums[0:1, :] += column_sum(g_fin * normal)
        sums[1:2, :] += column_sum(g_fin)
        g_enc = norm_back(g_fin, row_of(vec, FINAL_GAIN), normal, scale)
        low_enc = g_enc.astype(low)
        g_mlp[...] = low_enc
        sums[2:3, :] += column_sum(low_enc.astype(wide))
        back = jnp.zeros_like(g_enc)
        for part in range(fc1.shape[1] // width):
            cols = slice(part * width, (part + 1) * width)
            grad = (dot_nt(low_enc, fc2[cols, :]) * slope[:, cols].astype(wide)).astype(low)
            g_hidden[:, cols] = grad
            fc1_sum[0:1, cols] += column_sum(grad.astype(wide))
            back = back + dot_nt(grad, fc1[:, cols])
        normal, scale = normalise(res[...])
        sums[3:4, :] += column_sum(back * normal)
        sums[4:5, :] += column_sum(back)
        total = g_enc + norm_back(back, row_of(vec, NORM2_GAIN), normal, scale)
        g_res[...] = total
        low_res = total.astype(low)
        g_branch[...] = low_res
        sums[5:6, :] += column_sum(low_res.astype(wide))
        grad = dot_nt(low_res, attn_w[...]).astype(low)
        g_att[...] = grad
        top, rest = halves(grad.astype(wide) * att[...].astype(wide))
        delta[0] = dot_nt(spread[...], top) + dot_nt(spread[...], rest)


def back_call(
    sz, meta, fin, enc, res, att, slope, shares, lift, drop, probe_w, vec, attn_w, fc1, fc2
):
    w, f, n = sz.width, sz.hidden, sz.images
    lines = 8 * sz.pairs
    line = lax.broadcasted_iota(jnp.int32, (lines, w), 0)
    head = lax.broadcasted_iota(jnp.int32, (lines, w), 1) // HEAD_DIM
    spread = (head == 2 * (line // 8) + line % 8).astype(low)
    fixed = (probe_w, spread, vec, attn_w, fc1, fc2)

    def out(shape, dtype):
        return jax.ShapeDtypeStruct(shape, dtype)

    def kept(shape):
        return pl.BlockSpec(shape, lambda i, b, m: (0, 0))

    return pl.pallas_call(
        back_body,
        grid_spec=pltpu.PrefetchScalarGridSpec(
            num_scalar_prefetch=1,
            grid=(n, sz.blocks),
            in_specs=[
                sz.row_spec(w), sz.row_spec(w), sz.row_spec(w), sz.row_spec(w), sz.row_spec(f),
                sz.lane_spec(HEAD_ROWS), sz.image_spec(HEAD_ROWS, w), sz.image_spec(HEAD_ROWS, PAIR),
            ]
            + [whole(v.shape) for v in fixed],
            out_specs=[
                sz.row_spec(w), sz.row_spec(f), sz.row_spec(w), sz.row_spec(w), sz.row_spec(w),
                sz.lane_spec(lines), kept((HEAD_ROWS, w)), kept((8, w)), kept((8, f)),
            ],
        ),
        out_shape=[
            out((sz.rows, w), low), out((sz.rows, f), low), out((sz.rows, w), wide),
            out((sz.rows, w), low), out((sz.rows, w), low), out((n, lines, sz.length), wide),
            out((HEAD_ROWS, w), wide), out((8, w), wide), out((8, f), wide),
        ],
        compiler_params=params(2),
        cost_estimate=cost(
            sz.rows * w * (2 * w + 4 * f), sz.rows * (22 * w + 4 * f) + 4 * w * f
        ),
        name="mlp_back",
    )(meta, fin, enc, res, att, slope, shares, lift, drop, *fixed)


def outer_body(images, blocks, meta, a_ref, b_ref, out_ref, acc):
    span = blocks * BLOCK
    for i in range(images):
        for keys in range(blocks + 1):

            @pl.when(meta[i] == keys)
            def _(i=i, keys=keys):
                if keys:
                    rows = slice(i * span, i * span + keys * BLOCK)
                    term = dot_tn(a_ref[rows, :], b_ref[rows, :])
                else:
                    term = jnp.zeros(acc.shape, wide)
                if i > 0:
                    term = term + acc[...]
                if i < images - 1:
                    acc[...] = term
                else:
                    out_ref[...] = term.astype(out_ref.dtype)


def outer_call(sz, meta, a, b, tile_m, tile_n, name):
    m, n = a.shape[1], b.shape[1]
    return pl.pallas_call(
        functools.partial(outer_body, sz.images, sz.blocks),
        grid_spec=pltpu.PrefetchScalarGridSpec(
            num_scalar_prefetch=1,
            grid=(m // tile_m, n // tile_n),
            in_specs=[
                pl.BlockSpec((sz.rows, tile_m), lambda i, j, c: (0, i)),
                pl.BlockSpec((sz.rows, tile_n), lambda i, j, c: (0, j)),
            ],
            out_specs=pl.BlockSpec((tile_m, tile_n), lambda i, j, c: (i, j)),
            scratch_shapes=[pltpu.VMEM((tile_m, tile_n), wide)],
        ),
        out_shape=jax.ShapeDtypeStruct((m, n), low),
        compiler_params=params(2),
        cost_estimate=cost(2 * sz.rows * m * n, 2 * sz.rows * (m + n) + 2 * m * n),
        name=name,
    )(meta, a, b)


def attend_back_body(
    images, blocks, meta, q_ref, k_ref, v_ref, g_ref, lse_ref, delta_ref, dq_ref, dk_ref, dv_ref,
    dk_acc, dv_acc,
):
    at = pl.program_id(0)
    count, length = meta[at], meta[images + at]
    lane = lax.broadcasted_iota(jnp.int32, (BLOCK, PAIR), 1)
    first = lane < HEAD_DIM

    def keep(value, head):
        own = first if head == 0 else jnp.logical_not(first)
        zero = jnp.zeros_like(value[:BLOCK])
        return jnp.concatenate(
            [
                jnp.where(own, value[r : r + BLOCK], zero)
                for r in range(0, value.shape[0], BLOCK)
            ],
            axis=0,
        )

    def variant(keys_in):
        near = keys_in - BLOCK
        valid = lax.broadcasted_iota(jnp.int32, (BLOCK, BLOCK), 0) + near < length
        keys = k_ref[:keys_in, :]
        kept_keys = [keep(keys, head) for head in range(2)]
        values = v_ref[:keys_in, :]
        kept_values = [keep(values, head) for head in range(2)]
        dk_acc[:keys_in, :] = jnp.zeros((keys_in, PAIR), wide)
        dv_acc[:keys_in, :] = jnp.zeros((keys_in, PAIR), wide)

        @pl.loop(0, count)
        def _(step):
            rows = pl.ds(pl.multiple_of(step * BLOCK, BLOCK), BLOCK)
            q, g = q_ref[rows, :], g_ref[rows, :]
            dq = None
            for head in range(2):
                log = lse_ref[0, head : head + 1, rows]
                drop = delta_ref[0, head : head + 1, rows]
                score = dot_nt(kept_keys[head], q) * 0.125
                share = jnp.exp(score - log)
                if near:
                    share = jnp.concatenate(
                        [share[:near], jnp.where(valid, share[near:], 0.0)], axis=0
                    )
                else:
                    share = jnp.where(valid, share, 0.0)
                reach = dot_nt(kept_values[head], g)
                grad = (share * (reach - drop)).astype(low)
                dv_acc[:keys_in, :] += dot_nn(share.astype(low), keep(g, head))
                dk_acc[:keys_in, :] += dot_nn(grad, keep(q, head))
                term = dot_tn(grad, kept_keys[head])
                dq = term if dq is None else dq + term
            dq_ref[rows, :] = (dq * 0.125).astype(low)

        dk_ref[:keys_in, :] = (dk_acc[:keys_in, :] * 0.125).astype(low)
        dv_ref[:keys_in, :] = dv_acc[:keys_in, :].astype(low)

    for keys in range(1, blocks + 1):
        pl.when(count == keys)(functools.partial(variant, keys * BLOCK))


def attend_back_call(sz, meta, qkv, g_att, lse, delta):
    pairs = sz.pairs

    def spec(part):
        return pl.BlockSpec((sz.length, PAIR), lambda i, p, m: (i, part * pairs + p))

    line = pl.BlockSpec((1, 8, sz.length), lambda i, p, m: (i, p, 0))
    out = jax.ShapeDtypeStruct((sz.rows, sz.width), low)
    return pl.pallas_call(
        functools.partial(attend_back_body, sz.images, sz.blocks),
        grid_spec=pltpu.PrefetchScalarGridSpec(
            num_scalar_prefetch=1,
            grid=(sz.images, pairs),
            in_specs=[spec(0), spec(1), spec(2), spec(0), line, line],
            out_specs=[spec(0), spec(0), spec(0)],
            scratch_shapes=[pltpu.VMEM((sz.length, PAIR), wide)] * 2,
        ),
        out_shape=[out, out, out],
        compiler_params=params(2),
        cost_estimate=cost(
            10 * sz.rows * sz.length * sz.width,
            14 * sz.rows * sz.width,
            sz.rows * sz.length * HEADS,
        ),
        name="attend_back",
    )(meta, qkv, qkv, qkv, g_att, lse, delta)


def qkv_back_body(meta, x, g_res, dq, dk, dv, vec, weight, grad_ref, sums):
    @pl.when((pl.program_id(0) == 0) & (pl.program_id(1) == 0))
    def _():
        sums[...] = jnp.zeros_like(sums)

    live = pl.program_id(1) < meta[pl.program_id(0)]

    @pl.when(live)
    def _():
        width = x.shape[1]
        normal, scale = normalise(x[...].astype(wide))
        back = None
        for part, ref in enumerate((dq, dk, dv)):
            term = dot_nt(ref[...], weight[:, part * width : (part + 1) * width])
            back = term if back is None else back + term
        sums[0:1, :] += column_sum(back * normal)
        sums[1:2, :] += column_sum(back)
        sums[2:3, :] += column_sum(dq[...].astype(wide))
        sums[3:4, :] += column_sum(dv[...].astype(wide))
        grad_ref[...] = g_res[...] + norm_back(back, row_of(vec, NORM1_GAIN), normal, scale)

    @pl.when(jnp.logical_not(live))
    def _():
        grad_ref[...] = jnp.zeros_like(grad_ref)


def qkv_back_call(sz, meta, x, g_res, dq, dk, dv, vec, weight):
    w, blocks = sz.width, sz.blocks
    return pl.pallas_call(
        qkv_back_body,
        grid_spec=pltpu.PrefetchScalarGridSpec(
            num_scalar_prefetch=1,
            grid=(sz.images, blocks),
            in_specs=[sz.row_spec(w)] * 5 + [whole(vec.shape), whole(weight.shape)],
            out_specs=[
                pl.BlockSpec((BLOCK, w), lambda i, b, m: (i * blocks + b, 0)),
                pl.BlockSpec((8, w), lambda i, b, m: (0, 0)),
            ],
        ),
        out_shape=[
            jax.ShapeDtypeStruct((sz.rows, w), wide),
            jax.ShapeDtypeStruct((8, w), wide),
        ],
        compiler_params=params(2),
        cost_estimate=cost(6 * sz.rows * w * w, sz.rows * w * 16 + 6 * w * w),
        name="qkv_back",
    )(meta, x, g_res, dq, dk, dv, vec, weight)


axes = ("img", "seq")


def swap(value, bit, count):
    return lax.ppermute(value, axes, [(i, i ^ bit) for i in range(count)])


def bits_of(count):
    return [1 << k for k in range(count.bit_length() - 1)]


def small_gather(value, me, count):
    value = value[None]
    for bit in bits_of(count):
        other = swap(value, bit, count)
        value = jnp.where(
            (me & bit) > 0,
            jnp.concatenate([other, value], axis=0),
            jnp.concatenate([value, other], axis=0),
        )
    return value


def small_sum(value, count):
    for bit in bits_of(count):
        value = value + swap(value, bit, count)
    return value


def small_scatter(value, me, count):
    for bit in reversed(bits_of(count)):
        pair = value.reshape((2, value.shape[0] // 2) + value.shape[1:])
        up = (me & bit) > 0
        value = jnp.where(up, pair[1], pair[0]) + swap(
            jnp.where(up, pair[0], pair[1]), bit, count
        )
    return value[0]


def gathered(value):
    return lax.all_gather(value, axes, axis=0, tiled=True)


def scattered(value):
    return lax.psum_scatter(value, axes, scatter_dimension=0, tiled=True).astype(wide)


def local(img_count, seq_count, *args):
    (
        patches, lengths, pooled_cot, norm1_gain, norm1_bias, qkv_weight, query_bias, value_bias,
        attn_weight, attn_bias, norm2_gain, norm2_bias, fc1_weight, fc1_bias, fc2_weight, fc2_bias,
        final_gain, final_bias, probe_vector, pool_query_weight, pool_query_bias, pool_kv_weight,
        pool_value_bias, pool_out_weight, pool_out_bias, head_gain, head_bias, head_fc1_weight,
        head_fc1_bias, head_fc2_weight, head_fc2_bias,
    ) = args
    count = img_count * seq_count
    groups, part_rows, width = patches.shape
    length = part_rows * seq_count
    hidden = fc1_weight.shape[1]
    images = max(1, groups // seq_count)
    share = max(1, seq_count // groups)
    own = width // count
    fold = hidden // width
    sz = Sizes(images, length, width, hidden)
    me = lax.axis_index(axes)
    seq_at = lax.axis_index("seq")

    vectors = jnp.stack(
        [
            norm1_gain, norm1_bias, query_bias, value_bias, attn_bias, norm2_gain, norm2_bias,
            fc2_bias, final_gain, final_bias, pool_query_bias, pool_value_bias, pool_out_bias,
            head_gain, head_bias, head_fc2_bias,
        ]
        + [v for b in (fc1_bias, head_fc1_bias) for v in b.reshape(fold, own)]
    )
    vectors = small_gather(vectors, me, count).astype(wide)
    vec = vectors[:, :16].transpose(1, 0, 2).reshape(16, width)
    fcb = vectors[:, 16:].reshape(count, 2, fold * own).transpose(1, 0, 2).reshape(2, hidden)

    if seq_count > 1:
        x = lax.all_to_all(
            jnp.repeat(patches, share, axis=0), "seq", split_axis=0, concat_axis=1, tiled=True
        )
    else:
        x = patches
    x = x.reshape(sz.rows, width)
    first_image = (seq_at // share) * images
    own_lengths = lax.dynamic_slice_in_dim(lengths, first_image, images)
    own_lengths = jnp.where(seq_at % share == 0, own_lengths, 0)
    own_cot = lax.dynamic_slice_in_dim(pooled_cot, first_image, images)
    meta = jnp.concatenate([(own_lengths + BLOCK - 1) // BLOCK, own_lengths]).astype(jnp.int32)

    qkv_full = gathered(qkv_weight)
    attn_full = gathered(attn_weight)
    fc1_full = gathered(fc1_weight)
    fc2_full = gathered(fc2_weight)
    pool_k, pool_v = pool_kv_weight[:, :width], pool_kv_weight[:, width:]
    pool_v_full = gathered(pool_v)
    pool_out_full = gathered(pool_out_weight)
    head_fc1_full = gathered(head_fc1_weight)
    head_fc2_full = gathered(head_fc2_weight)

    query_part = jnp.sum(
        probe_vector.astype(wide)[:, None] * pool_query_weight.astype(wide), axis=0, keepdims=True
    )
    pool_query = (small_sum(query_part, count) + vec[POOL_QUERY_BIAS:][:1]).astype(low)
    pool_query = pool_query.astype(wide)
    probe_own = (pool_k.astype(wide) * pool_query).reshape(own, HEADS, HEAD_DIM).sum(-1) * 0.125
    probe_own = jnp.pad(probe_own, ((0, 0), (0, HEAD_ROWS - HEADS)))
    probe_w = small_gather(probe_own.T, me, count).transpose(1, 0, 2).reshape(HEAD_ROWS, width)

    qkv, n1 = qkv_call(sz, meta, x, vec, qkv_full)
    att, lse = attend_call(sz, meta, qkv)
    res, n2, slope, act, enc, fin = mlp_call(
        sz, meta, x, att, vec, fcb, attn_full, fc1_full, fc2_full
    )
    cot_rows = jnp.pad(own_cot, ((0, HEAD_ROWS - images), (0, 0)))
    pooled, shares, lift, drop, mixed, wide_rows, narrow_rows, head_sums = head_call(
        sz, meta, fin, probe_w, cot_rows, vec, fcb, pool_v_full, pool_out_full, head_fc1_full,
        head_fc2_full,
    )
    pooled = lax.all_gather(pooled[:images], "seq", axis=0, tiled=True)[::share]

    g_mlp, g_hidden, g_res, g_branch, g_att, delta, mix, back_sums, fc1_sum = back_call(
        sz, meta, fin, enc, res, att, slope, shares, lift, drop, probe_w, vec, attn_full,
        fc1_full, fc2_full,
    )
    grad_fc2 = scattered(outer_call(sz, meta, act, g_mlp, 768, width, "grad_fc2"))
    grad_fc1 = scattered(outer_call(sz, meta, n2, g_hidden, width, 768, "grad_fc1"))
    grad_attn = scattered(outer_call(sz, meta, att, g_branch, width, 768, "grad_attn"))
    dq, dk, dv = attend_back_call(sz, meta, qkv, g_att, lse, delta)
    patch_grad, qkv_sums = qkv_back_call(sz, meta, x, g_res, dq, dk, dv, vec, qkv_full)
    grad_qkv = jnp.concatenate(
        [
            outer_call(sz, meta, n1, d, width, 768, "grad_" + name)
            for d, name in ((dq, "q"), (dk, "k"), (dv, "v"))
        ],
        axis=1,
    )
    grad_qkv = scattered(grad_qkv)

    def chunks(v, per):
        return v.reshape(v.shape[0], count, per).transpose(1, 0, 2)

    sent = jnp.concatenate(
        [
            chunks(narrow_rows[:images, :hidden], hidden // count),
            chunks(narrow_rows[:images, hidden : hidden + width], own),
            chunks(narrow_rows[:images, hidden + width :], own),
            mixed[:, :HEADS].reshape(images, HEADS, count, own).transpose(2, 0, 1, 3).reshape(
                count, images, HEADS * own
            ),
        ],
        axis=2,
    )
    mine = lax.all_to_all(sent, axes, split_axis=0, concat_axis=0, tiled=True)
    mine = mine.reshape(count * images, -1)
    rows = small_gather(wide_rows[:images], me, count).reshape(count * images, -1)
    per = hidden // count
    act_own, normed_own = mine[:, :per], mine[:, per : per + own]
    pooled_own, mixed_own = mine[:, per + own : per + 2 * own], mine[:, per + 2 * own :]
    head_grad, branch_rows = rows[:, :hidden], rows[:, hidden : hidden + width]
    pooled_rows, cot_all = rows[:, hidden + width : hidden + 2 * width], rows[:, hidden + 2 * width :]
    grad_head_fc2 = dot_tn(act_own, cot_all)
    grad_head_fc1 = dot_tn(normed_own, head_grad)
    grad_pool_out = dot_tn(pooled_own, branch_rows)
    grad_pool_v = jnp.einsum(
        "ihr,ihd->rhd",
        mixed_own.reshape(-1, HEADS, own),
        pooled_rows.reshape(-1, HEADS, HEAD_DIM),
        preferred_element_type=wide,
    ).reshape(own, width)
    row_sums = jnp.sum(rows.astype(wide), axis=0)
    mix_own = small_scatter(
        mix[:HEADS].reshape(HEADS, count, own).transpose(1, 0, 2), me, count
    )
    grad_pool_k = (
        0.125 * mix_own.T[:, :, None] * pool_query.reshape(1, HEADS, HEAD_DIM)
    ).reshape(own, width)
    query_grad = 0.125 * jnp.sum(
        mix_own.T[:, :, None] * pool_k.astype(wide).reshape(own, HEADS, HEAD_DIM), axis=0
    )
    query_grad = small_sum(query_grad.reshape(1, width), count)
    grad_pool_query_weight = probe_vector.astype(wide)[:, None] * query_grad
    grad_probe = jnp.sum(pool_query_weight.astype(wide) * query_grad, axis=1)
    grad_pool_kv = jnp.concatenate([grad_pool_k, grad_pool_v], axis=1)

    sums = jnp.concatenate([back_sums[:6], head_sums[:2], qkv_sums[:4]], axis=0)
    sums = jnp.concatenate(
        [
            sums.reshape(12, count, own).transpose(1, 0, 2).reshape(count, 12 * own),
            fc1_sum[0].reshape(count, per),
        ],
        axis=1,
    )
    sums = small_scatter(sums, me, count)
    (
        g_final_gain, g_final_bias, g_fc2_bias, g_norm2_gain, g_norm2_bias, g_attn_bias,
        g_head_gain, g_head_bias, g_norm1_gain, g_norm1_bias, g_query_bias, g_value_bias,
    ) = sums[: 12 * own].reshape(12, own)
    g_fc1_bias = sums[12 * own :]

    def own_part(v, size):
        return lax.dynamic_slice_in_dim(v, me * size, size)

    g_head_fc1_bias = own_part(row_sums[:hidden], per)
    g_pool_out_bias = own_part(row_sums[hidden : hidden + width], own)
    g_pool_value_bias = own_part(row_sums[hidden + width : hidden + 2 * width], own)
    g_head_fc2_bias = own_part(row_sums[hidden + 2 * width :], own)
    g_pool_query_bias = own_part(query_grad[0], own)

    patch_grad = patch_grad.reshape(images, length, width)
    if seq_count > 1:
        back = lax.all_to_all(
            patch_grad.astype(low), "seq", split_axis=1, concat_axis=0, tiled=True
        )[::share].astype(wide)
        if share == 1:
            kept = lax.dynamic_slice_in_dim(patch_grad, seq_at * part_rows, part_rows, axis=1)
            back = lax.dynamic_update_slice_in_dim(back, kept, first_image, axis=0)
        patch_grad = back
    return (
        pooled, patch_grad, g_norm1_gain, g_norm1_bias, grad_qkv, g_query_bias, g_value_bias,
        grad_attn, g_attn_bias, g_norm2_gain, g_norm2_bias, grad_fc1, g_fc1_bias, grad_fc2,
        g_fc2_bias, g_final_gain, g_final_bias, grad_probe, grad_pool_query_weight,
        g_pool_query_bias, grad_pool_kv, g_pool_value_bias, grad_pool_out, g_pool_out_bias,
        g_head_gain, g_head_bias, grad_head_fc1, g_head_fc1_bias, grad_head_fc2, g_head_fc2_bias,
    )


def solution(mesh):
    rows, vector = P(axes, None), P(axes)
    body = functools.partial(local, mesh.shape["img"], mesh.shape["seq"])
    vector_weights = (3, 4, 6, 7, 9, 10, 11, 13, 15, 16, 17, 18, 20, 22, 24, 25, 26, 28, 30)
    in_specs = (P("img", "seq", None), P("img"), P("img", None)) + tuple(
        vector if at in vector_weights else rows for at in range(3, 31)
    )
    out_specs = (P("img", None), P("img", "seq", None)) + in_specs[3:]
    return jax.shard_map(body, mesh=mesh, in_specs=in_specs, out_specs=out_specs, check_vma=False)
```

time: 2640 us -> 1030 us (0.39)
  waiting for transfers between devices: 1630 us -> 591 us
  matrix products: 553 us -> 6.76 us
  Pallas kernels: 0 us -> 206 us
  local copies, waits for them, and re-layouts: 193 us -> 51.1 us
  other arithmetic: 175 us -> 34.7 us
  starting transfers between devices: 1.63 us -> 115 us
  blocking collectives: 57.3 us -> 4.36 us
    reduce_scatter x11 -> x4, waiting for transfers between devices: 1230 us -> 176 us  [scattered(): lax.psum_scatter(value, axes, scatter_dimension=0, tiled=True).astype(wide)]
    dot_general x58 -> x4, matrix products: 553 us -> 6.76 us  [the longest x3 5.69 us: dot_tn(): lax.dot_general(a, b, (((0,), (0,)), ((), ())), preferred_element_type=wide)]
    pallas_call x0 -> x13, Pallas kernels: none -> 206 us  [the longest x6 50.6 us: outer_call(): pl.pallas_call(functools.partial(outer_body, sz.images, sz.blocks), grid_...]
    ppermute x0 -> x35, starting transfers between devices: none -> 102 us  [swap(): return lax.ppermute(value, axes, [(i, i ^ bit) for i in range(count)])]
    ppermute x0 -> x35, waiting for transfers between devices: none -> 76 us  [swap(): return lax.ppermute(value, axes, [(i, i ^ bit) for i in range(count)])]
    convert_element_type x29 -> x8, other arithmetic: 85.3 us -> 11.1 us  [the longest x4 6.29 us: scattered(): lax.psum_scatter(value, axes, scatter_dimension=0, tiled=True).astype(wide)]
    reduce_sum x20 -> x4, other arithmetic: 73.4 us -> 5.38 us  [the longest x1 3.62 us: local(): row_sums = jnp.sum(rows.astype(wide), axis=0)]
    unnamed x243 -> x72, local copies, waits for them, and re-layouts: 64 us -> 2.85 us
  transfers between devices with their start and end apart: 23 -> 50, of which waited for: 19 -> 26; matrix products, arithmetic and copies ran while one was open for 16% -> 9% of each run, Pallas kernels for 0% -> 15%
where the time goes in v1:
time: 1030 us; the launch traced here: 1020 us
  waiting for transfers between devices  591 us (57%)
  Pallas kernels  206 us (20%)
  starting transfers between devices  115 us (11%)
  local copies, waits for them, and re-layouts  51.1 us (5%)
  other arithmetic  34.7 us (3%)
  between operations  15.7 us (2%)
    all_gather x8, waiting for transfers between devices, gathered(): return lax.all_gather(value, axes, axis=0, tiled=True)  328 us
    reduce_scatter x4, waiting for transfers between devices, scattered(): lax.psum_scatter(value, axes, scatter_dimension=0, tiled=True).astype(wide)  176 us
    ppermute x35, starting transfers between devices, swap(): return lax.ppermute(value, axes, [(i, i ^ bit) for i in range(count)])  102 us
    ppermute x35, waiting for transfers between devices, swap(): return lax.ppermute(value, axes, [(i, i ^ bit) for i in range(count)])  76 us
    pallas_call x6, Pallas kernels, outer_call(): pl.pallas_call(functools.partial(outer_body, sz.images, sz.blocks), grid_...  50.6 us
    pallas_call x1, Pallas kernels, back_call(): pl.pallas_call(back_body, grid_spec=pltpu.PrefetchScalarGridSpec(num_scal...  33.9 us
    pallas_call x1, Pallas kernels, mlp_call(): pl.pallas_call(mlp_body, grid_spec=pltpu.PrefetchScalarGridSpec(num_scala...  28.4 us
    pallas_call x1, Pallas kernels, attend_back_call(): pl.pallas_call(functools.partial(attend_back_body, sz.images, sz.blocks),...  27.5 us
  transfers between devices with their start and end apart: 50, of which 26 were waited for; matrix products, arithmetic and copies ran while one was open for 9% of the time, Pallas kernels for 15%

profile of v1, /device:TPU:0, one launch (start us, length us, event | category | flops | bytes accessed | tf_op | source)
XLA Modules:
  0.0 1024.5 jit_solution(7055093462819524596)
XLA Ops:
  13.8 4.2 all-to-all-start
  22.2 35.7 %collective-permute-done = bf16[1,24,24]{2,1,0:T(8,128)(2,1)S(1)} collective-permute-done((bf16[1,24,24]{2,1,0:T(8,128)(2,1)S(1)}, bf16[1,24,24]{2,1,0:T(8,128)(2,1)S(1)}, u32[]{:S(2)}, u32[]{:S(2)}) %collective-permute-start) | collective-permute-done | bytes 1184 | tf_op jit(solution)/shard_map/ppermute | solution.py:691
  72.3 5.2 collective-permute-done.4
  109.8 6.4 collective-permute-done.14
  120.1 11.3 %qkv.1 = (bf16[2048,2304]{1,0:T(8,128)(2,1)}, bf16[2048,768]{1,0:T(8,128)(2,1)}) custom-call(s32[4]{0:T(128)} %pad_add_fusion.meta, bf16[2048,768]{1,0:T(8,128)(2,1)} %bitcast.116, f32[16,768]{1,0:T(8,128)} %reshape.243.vec, bf16[768,2304]{1,0:T(8,128)(2,1)} %all-gather.10.cloned.1.call-done.weight), custom_call_target="tpu_custom_call" | custom-call | flops 7247757312 | bytes 19267584 | tf_op jit(solution)/shard_map/qkv/pallas_call | solution.py:141
  131.4 22.6 %attend.1 = (bf16[2048,768]{1,0:T(8,128)(2,1)}, f32[2,48,1024]{2,1,0:T(8,128)}) custom-call(s32[4]{0:T(128)} %pad_add_fusion.meta, bf16[2048,2304]{1,0:T(8,128)(2,1)} %get-tuple-element.62.q_ref.k_ref.v_ref, bf16[2048,2304]{1,0:T(8,128)(2,1)} %get-tuple-element.62.q_ref.k_ref.v_ref, bf16[2048,2304]{1,0:T(8,128)(2,1)} %get-tuple-element.62.q_ref.k_ref.v_ref), custom_call_target="tpu_custom_call" | custom-call | flops 6442450944 | bytes 12582912 | tf_op jit(solution)/shard_map/attend/pallas_call | solution.py:206
  154.0 47.6 %all-gather.14.cloned.1.call-done.fc1 = bf16[768,3072]{1,0:T(8,128)(2,1)} async-done(((bf16[24,3072]{1,0:T(8,128)(2,1)}), bf16[768,3072]{1,0:T(8,128)(2,1)}) %all-gather.14.cloned.1.call-update) | async-done | bytes 4718608 | tf_op jit(solution)/shard_map/all_gather | solution.py:727
  201.6 65.3 %all-gather.16.cloned.1.call-done.fc2 = bf16[3072,768]{1,0:T(8,128)(2,1)} async-done(((bf16[96,768]{1,0:T(8,128)(2,1)}), bf16[3072,768]{1,0:T(8,128)(2,1)}) %all-gather.16.cloned.1.call-update) | async-done | bytes 4718608 | tf_op jit(solution)/shard_map/all_gather | solution.py:727
  266.9 28.4 %mlp.1 = (f32[2048,768]{1,0:T(8,128)}, bf16[2048,768]{1,0:T(8,128)(2,1)}, bf16[2048,3072]{1,0:T(8,128)(2,1)}, bf16[2048,3072]{1,0:T(8,128)(2,1)}, f32[2048,768]{1,0:T(8,128)}, /*index=5*/bf16[2048,768]{1,0:T(8,128)(2,1)}) custom-call(s32[4]{0:T(128)} %pad_add_fusion.meta, bf16[2048,768]{1,0:T(8,128)(2,1)} %bitcast.117, ...), custom_call_target="tpu_custom_call" | custom-call | flops 21743271936 | bytes 56623104 | tf_op jit(solution)/shard_map/mlp/pallas_call | solution.py:262
  295.2 27.4 %all-gather.20.cloned.1.call-done.pool_out = bf16[768,768]{1,0:T(8,128)(2,1)} async-done(((bf16[24,768]{1,0:T(8,128)(2,1)}), bf16[768,768]{1,0:T(8,128)(2,1)}) %all-gather.20.cloned.1.call-update) | async-done | bytes 1179664 | tf_op jit(solution)/shard_map/all_gather | solution.py:727
  322.6 56.5 %all-gather.18.cloned.1.call-done.pool_v = bf16[768,768]{1,0:T(8,128)(2,1)} async-done(((bf16[24,768]{1,0:T(8,128)(2,1)}), bf16[768,768]{1,0:T(8,128)(2,1)}) %all-gather.18.cloned.1.call-update) | async-done | bytes 1179664 | tf_op jit(solution)/shard_map/all_gather | solution.py:727
  379.1 65.5 %all-gather.22.cloned.1.call-done.fc1 = bf16[768,3072]{1,0:T(8,128)(2,1)} async-done(((bf16[24,3072]{1,0:T(8,128)(2,1)}), bf16[768,3072]{1,0:T(8,128)(2,1)}) %all-gather.22.cloned.1.call-update) | async-done | bytes 4718608 | tf_op jit(solution)/shard_map/all_gather | solution.py:727
  444.6 65.4 %all-gather.24.cloned.1.call-done.fc2 = bf16[3072,768]{1,0:T(8,128)(2,1)} async-done(((bf16[96,768]{1,0:T(8,128)(2,1)}), bf16[3072,768]{1,0:T(8,128)(2,1)}) %all-gather.24.cloned.1.call-update) | async-done | bytes 4718608 | tf_op jit(solution)/shard_map/all_gather | solution.py:727
  510.0 16.9 %head.1 = (f32[16,768]{1,0:T(8,128)}, f32[2,16,1024]{2,1,0:T(8,128)}, f32[2,16,768]{2,1,0:T(8,128)}, f32[2,16,128]{2,1,0:T(8,128)}, bf16[2,16,768]{2,1,0:T(8,128...) custom-call(s32[4]{0:T(128)} %pad_add_fusion.meta, ...), custom_call_target="tpu_custom_call" | custom-call | flops 301989888 | bytes 14942208 | tf_op jit(solution)/shard_map/head/pallas_call | solution.py:393
  526.9 33.9 %mlp_back.1 = (bf16[2048,768]{1,0:T(8,128)(2,1)}, bf16[2048,3072]{1,0:T(8,128)(2,1)}, f32[2048,768]{1,0:T(8,128)}, bf16[2048,768]{1,0:T(8,128)(2,1)}, bf16[2048,...) custom-call(s32[4]{0:T(128)} %pad_add_fusion.meta, ...), custom_call_target="tpu_custom_call" | custom-call | flops 21743271936 | bytes 69206016 | tf_op jit(solution)/shard_map/mlp_back/pallas_call | solution.py:480
  560.8 6.4 grad_attn.1
  567.3 27.5 %attend_back.1 = (bf16[2048,768]{1,0:T(8,128)(2,1)}, bf16[2048,768]{1,0:T(8,128)(2,1)}, bf16[2048,768]{1,0:T(8,128)(2,1)}) custom-call(s32[4]{0:T(128)} %pad_add_fusion.meta, bf16[2048,2304]{1,0:T(8,128)(2,1)} %get-tuple-element.62.q_ref.k_ref.v_ref, bf16[2048,2304]{1,0:T(8,128)(2,1)} %get-tuple-element.62.q_ref.k_ref.v_ref, ...), custom_call_target="tpu_custom_call" | custom-call | flops 16106127360 | bytes 22020096 | tf_op jit(solution)/shard_map/attend_back/pallas_call | solution.py:618
  594.7 6.7 grad_v.1
  601.4 6.3 grad_k.1
  607.7 6.6 grad_q.1
  617.3 12.2 %grad_fc2.1 = bf16[3072,768]{1,0:T(8,128)(2,1)} custom-call(s32[4]{0:T(128)} %pad_add_fusion.meta, bf16[2048,3072]{1,0:T(8,128)(2,1)} %get-tuple-element.88.a_ref, bf16[2048,768]{1,0:T(8,128)(2,1)} %get-tuple-element.89.b_ref), custom_call_target="tpu_custom_call" | custom-call | flops 9663676416 | bytes 20447232 | tf_op jit(solution)/shard_map/grad_fc2/pallas_call | solution.py:530
  630.3 14.9 %qkv_back.1 = (f32[2048,768]{1,0:T(8,128)}, f32[8,768]{1,0:T(8,128)}) custom-call(s32[4]{0:T(128)} %pad_add_fusion.meta, bf16[2048,768]{1,0:T(8,128)(2,1)} %bitcast.118, f32[2048,768]{1,0:T(8,128)} %get-tuple-element.72.g_res, bf16[2048,768]{1,0:T(8,128)(2,1)} %get-tuple-element.76.dq.b_ref, bf16[2048,768]{1,0:T(8,128)(2,1)} %get-tuple-element.77.dk.b_ref, ...), custom_call_target="tpu_custom_call" | custom-call | flops 7247757312 | bytes 28704768 | tf_op jit(solution)/shard_map/qkv_back/pallas_call | solution.py:666
  647.6 42.6 %collective-permute-start.20 = (f32[16,12,24]{1,2,0:T(8,128)S(1)}, f32[16,12,24]{1,2,0:T(8,128)S(1)}, u32[]{:S(2)}, u32[]{:S(2)}) collective-permute-start(f32[16,12,24]{1,2,0:T(8,128)S(1)} %slice_select_fusion), channel_id=1, source_target_pairs={{0,16},{1,17},{2,18},{3,19},{4,20},{5,21},{6,22},{7,23},{8,24},{9,... | collective-permute-start | bytes 55304 | tf_op jit(solution)/shard_map/ppermute | solution.py:691
  693.5 4.4 all-gather
  701.9 22.6 %collective-permute-start.21 = (f32[8,12,24]{1,2,0:T(8,128)S(1)}, f32[8,12,24]{1,2,0:T(8,128)S(1)}, u32[]{:S(2)}, u32[]{:S(2)}) collective-permute-start(f32[8,12,24]{1,2,0:T(8,128)S(1)} %slice_select_fusion.1), channel_id=1, source_target_pairs={{0,8},{1,9},{2,10},{3,11},{4,12},{5,13},{6,14},{7,15},{8,0},{9,1},... | collective-permute-start | bytes 27656 | tf_op jit(solution)/shard_map/ppermute | solution.py:691
  725.3 4.6 all-to-all-start.2
  732.1 12.5 %grad_fc1.1 = bf16[768,3072]{1,0:T(8,128)(2,1)} custom-call(s32[4]{0:T(128)} %pad_add_fusion.meta, bf16[2048,768]{1,0:T(8,128)(2,1)} %get-tuple-element.86.a_ref, bf16[2048,3072]{1,0:T(8,128)(2,1)} %get-tuple-element.87.b_ref), custom_call_target="tpu_custom_call" | custom-call | flops 9663676416 | bytes 20447232 | tf_op jit(solution)/shard_map/grad_fc1/pallas_call | solution.py:530
  744.6 9.4 copy.147
  791.4 3.9 all-to-all-start.1
  818.9 6.5 all-to-all-done.1
  837.8 65.3 %reduce-scatter.11.cloned.1.call-done = bf16[96,768]{1,0:T(8,128)(2,1)} async-done(((bf16[3072,768]{1,0:T(8,128)(2,1)}), bf16[96,768]{1,0:T(8,128)(2,1)}) %reduce-scatter.11.cloned.1.call-update) | async-done | bytes 147472 | tf_op jit(solution)/shard_map/reduce_scatter | solution.py:731
  904.7 110.7 %reduce-scatter.9.cloned.1.call-done = bf16[24,3072]{1,0:T(8,128)(2,1)} async-done(((bf16[768,3072]{1,0:T(8,128)(2,1)}), bf16[24,3072]{1,0:T(8,128)(2,1)}) %reduce-scatter.9.cloned.1.call-update) | async-done | bytes 147472 | tf_op jit(solution)/shard_map/reduce_scatter | solution.py:731
  (306 shorter events, 153.4 us)
Async XLA Ops:
  7.2 112.9 %all-gather.10.cloned.1.call-start = ((), (), s32[]{:S(2)}) async-start(), calls=%async_computation.7 | async-start | bytes 3649536 | tf_op jit(solution)/shard_map/all_gather | solution.py:727
  8.0 146.0 %all-gather.12.cloned.1.call-start = ((), (), s32[]{:S(2)}) async-start(), calls=%async_computation.8 | async-start | bytes 1216512 | tf_op jit(solution)/shard_map/all_gather | solution.py:727
  8.9 192.7 %all-gather.14.cloned.1.call-start = ((), (), s32[]{:S(2)}) async-start(), calls=%async_computation.9 | async-start | bytes 4866048 | tf_op jit(solution)/shard_map/all_gather | solution.py:727
  9.7 257.2 %all-gather.16.cloned.1.call-start = ((), (), s32[]{:S(2)}) async-start(), calls=%async_computation.10 | async-start | bytes 4866048 | tf_op jit(solution)/shard_map/all_gather | solution.py:727
  10.2 312.4 %all-gather.20.cloned.1.call-start = ((), (), s32[]{:S(2)}) async-start(), calls=%async_computation.12 | async-start | bytes 1216512 | tf_op jit(solution)/shard_map/all_gather | solution.py:727
  10.8 368.3 %all-gather.18.cloned.1.call-start = ((), (), s32[]{:S(2)}) async-start(), calls=%async_computation.11 | async-start | bytes 1216512 | tf_op jit(solution)/shard_map/all_gather | solution.py:727
  12.3 432.3 %all-gather.22.cloned.1.call-start = ((), (), s32[]{:S(2)}) async-start(), calls=%async_computation.13 | async-start | bytes 4866048 | tf_op jit(solution)/shard_map/all_gather | solution.py:727
  13.0 497.0 %all-gather.24.cloned.1.call-start = ((), (), s32[]{:S(2)}) async-start(), calls=%async_computation.14 | async-start | bytes 4866048 | tf_op jit(solution)/shard_map/all_gather | solution.py:727
  13.8 104.4 %all-to-all-start = ((bf16[4,512,768]{2,1,0:T(8,128)(2,1)}), bf16[4,512,768]{2,1,0:T(8,128)(2,1)S(1)}, u32[]{:S(2)}, u32[]{:S(2)}) async-start(bf16[4,512,768]{2,1,0:T(8,128)(2,1)} %param.31), calls=%async_computation | async-start | bytes 6291456 | tf_op jit(solution)/shard_map/all_to_all | solution.py:767
  18.0 812.9 %reduce-scatter.7.cloned.1.call-start = ((), (), s32[]{:S(2)}) async-start(), calls=%async_computation.16 | async-start | bytes 1216512 | tf_op jit(solution)/shard_map/reduce_scatter | solution.py:731
  18.2 39.8 %collective-permute-start.5 = (f32[1,768]{1,0:T(1,128)S(1)}, f32[1,768]{1,0:T(1,128)S(1)}, u32[]{:S(2)}, u32[]{:S(2)}) collective-permute-start(f32[1,768]{1,0:T(1,128)S(1)} %broadcast_in_dim.22), channel_id=1, source_target_pairs={{0,1},{1,0},{2,3},{3,2},{4,5},{5,4},{6,7},{7,6},{8,9},{9,8},{10,11... | collective-permute-start | bytes 9224 | tf_op jit(solution)/shard_map/ppermute | solution.py:691
  21.3 36.5 %collective-permute-start = (bf16[1,24,24]{2,1,0:T(8,128)(2,1)S(1)}, bf16[1,24,24]{2,1,0:T(8,128)(2,1)S(1)}, u32[]{:S(2)}, u32[]{:S(2)}) collective-permute-start(bf16[1,24,24]{2,1,0:T(8,128)(2,1)S(1)} %bitcast.132), channel_id=1, source_target_pairs={{0,1},{1,0},{2,3},{3,2},{4,5},{5,4},{6,7},{7,6},{8,9},{9,8},{10,11... | collective-permute-start | bytes 3464 | tf_op jit(solution)/shard_map/ppermute | solution.py:691
  65.9 5.6 collective-permute-start.8
  68.1 9.4 collective-permute-start.4
  71.6 9.8 collective-permute-start.9
  103.9 12.3 %collective-permute-start.14 = (f32[16,16,24]{1,2,0:T(8,128)}, f32[16,16,24]{1,2,0:T(8,128)}, u32[]{:S(2)}, u32[]{:S(2)}) collective-permute-start(f32[16,16,24]{1,2,0:T(8,128)} %maximum_select_fusion.2), channel_id=1, source_target_pairs={{0,16},{1,17},{2,18},{3,19},{4,20},{5,21},{6,22},{7,23},{8,24},{9,... | collective-permute-start | bytes 73736 | tf_op jit(solution)/shard_map/ppermute | solution.py:691
  567.2 268.9 %reduce-scatter.5.cloned.1.call-start = ((), (), s32[]{:S(2)}) async-start(), calls=%async_computation.15 | async-start | bytes 3649536 | tf_op jit(solution)/shard_map/reduce_scatter | solution.py:731
  617.3 285.8 %reduce-scatter.11.cloned.1.call-start = ((), (), s32[]{:S(2)}) async-start(), calls=%async_computation.18 | async-start | bytes 4866048 | tf_op jit(solution)/shard_map/reduce_scatter | solution.py:731
  647.6 54.2 %collective-permute-start.20 = (f32[16,12,24]{1,2,0:T(8,128)S(1)}, f32[16,12,24]{1,2,0:T(8,128)S(1)}, u32[]{:S(2)}, u32[]{:S(2)}) collective-permute-start(f32[16,12,24]{1,2,0:T(8,128)S(1)} %slice_select_fusion), channel_id=1, source_target_pairs={{0,16},{1,17},{2,18},{3,19},{4,20},{5,21},{6,22},{7,23},{8,24},{9,... | collective-permute-start | bytes 55304 | tf_op jit(solution)/shard_map/ppermute | solution.py:691
  698.9 68.1 %collective-permute-start.30 = (bf16[1,2,5376]{2,1,0:T(2,128)(2,1)S(1)}, bf16[1,2,5376]{2,1,0:T(2,128)(2,1)S(1)}, u32[]{:S(2)}, u32[]{:S(2)}) collective-permute-start(bf16[1,2,5376]{2,1,0:T(2,128)(2,1)S(1)} %slice_bitcast_fusion.1), channel_id=1, source_target_pairs={{0,1},{1,0},{2,3},{3,2},{4,5},{5,4},{6,7},{7,6},{8,9},{9,8},{10,11... | collective-permute-start | bytes 64520 | tf_op jit(solution)/shard_map/ppermute | solution.py:691
  699.1 56.7 %collective-permute-start.15 = (f32[16,384]{1,0:T(8,128)S(1)}, f32[16,384]{1,0:T(8,128)S(1)}, u32[]{:S(2)}, u32[]{:S(2)}) collective-permute-start(f32[16,384]{1,0:T(8,128)S(1)} %broadcast_select_fusion.5), channel_id=1, source_target_pairs={{0,16},{1,17},{2,18},{3,19},{4,20},{5,21},{6,22},{7,23},{8,24},{9,... | collective-permute-start | bytes 73736 | tf_op jit(solution)/shard_map/ppermute | solution.py:691
  701.9 28.4 %collective-permute-start.21 = (f32[8,12,24]{1,2,0:T(8,128)S(1)}, f32[8,12,24]{1,2,0:T(8,128)S(1)}, u32[]{:S(2)}, u32[]{:S(2)}) collective-permute-start(f32[8,12,24]{1,2,0:T(8,128)S(1)} %slice_select_fusion.1), channel_id=1, source_target_pairs={{0,8},{1,9},{2,10},{3,11},{4,12},{5,13},{6,14},{7,15},{8,0},{9,1},... | collective-permute-start | bytes 27656 | tf_op jit(solution)/shard_map/ppermute | solution.py:691
  725.3 65.5 %all-to-all-start.2 = ((bf16[32,2,432]{2,1,0:T(2,128)(2,1)}), bf16[32,2,432]{2,1,0:T(2,128)(2,1)S(1)}, u32[]{:S(2)}, u32[]{:S(2)}) async-start(bf16[32,2,432]{2,1,0:T(2,128)(2,1)} %copy.138), calls=%async_computation.6 | async-start | bytes 131072 | tf_op jit(solution)/shard_map/all_to_all | solution.py:842
  730.0 285.5 %reduce-scatter.9.cloned.1.call-start = ((), (), s32[]{:S(2)}) async-start(), calls=%async_computation.17 | async-start | bytes 4866048 | tf_op jit(solution)/shard_map/reduce_scatter | solution.py:731
  730.3 23.7 %collective-permute-start.22 = (f32[4,12,24]{1,2,0:T(8,128)S(1)}, f32[4,12,24]{1,2,0:T(8,128)S(1)}, u32[]{:S(2)}, u32[]{:S(2)}) collective-permute-start(f32[4,12,24]{1,2,0:T(8,128)S(1)} %slice_select_fusion.2), channel_id=1, source_target_pairs={{0,4},{1,5},{2,6},{3,7},{4,0},{5,1},{6,2},{7,3},{8,12},{9,13},{10,... | collective-permute-start | bytes 13832 | tf_op jit(solution)/shard_map/ppermute | solution.py:691
  767.1 6.6 collective-permute-start.31
  768.2 5.5 collective-permute-start.19
  771.5 9.0 collective-permute-start.28
  778.9 6.0 collective-permute-start.33
  780.6 8.3 collective-permute-start.29
  785.7 14.8 %collective-permute-start.34 = (bf16[16,2,5376]{2,1,0:T(2,128)(2,1)S(1)}, bf16[16,2,5376]{2,1,0:T(2,128)(2,1)}, u32[]{:S(2)}, u32[]{:S(2)}) collective-permute-start(bf16[16,2,5376]{2,1,0:T(2,128)(2,1)S(1)} %broadcast_select_fusion.1), channel_id=1, source_target_pairs={{0,16},{1,17},{2,18},{3,19},{4,20},{5,21},{6,22},{7,23},{8,24},{9,... | collective-permute-start | bytes 1032200 | tf_op jit(solution)/shard_map/ppermute | solution.py:691
  791.4 34.0 %all-to-all-start.1 = ((bf16[2,1024,768]{2,0,1:T(2,128)(2,1)}), bf16[2,1024,768]{2,0,1:T(2,128)(2,1)S(1)}, u32[]{:S(2)}, u32[]{:S(2)}) async-start(bf16[2,1024,768]{2,0,1:T(2,128)(2,1)} %copy.147), calls=%async_computation.1 | async-start | bytes 6291456 | tf_op jit(solution)/shard_map/all_to_all | solution.py:900
  (53 other events, 789.4 us)
Sparse Core Ops, SparseCore 0:
  11.0 67.3 all-gather.9
  81.2 54.7 all-gather.11
  139.0 62.5 all-gather.13
  204.4 62.4 all-gather.15
  269.6 52.9 all-gather.19
  326.0 53.0 all-gather.17
  382.0 62.5 all-gather.21
  447.5 62.4 all-gather.23
  567.3 111.9 reduce-scatter.6
  684.6 103.7 reduce-scatter.4
  793.9 109.1 reduce-scatter.10
  909.3 106.0 reduce-scatter.8
